TPU v7x, 512 devices: a whole 4x4x16 slice. The times are simulated.
512 devices in a mesh: row: 32 (over x, y, core), col: 16 (over z).
Axes of the slice: x: 4, y: 4, z: 16, core: 2. Of those that a mesh axis runs over, the one named last changes fastest.
Arguments:
- panel: bfloat16 [4, 32, 512, 512], P(None, 'row', 'col'), may hold values from -1.25 to 1.25
- diagonal_tile: float32 [512, 512], P('row', 'col'), may hold values from 0 to 2.5, as said below
- trailing: bfloat16 [4, 32, 512, 16, 512], P(None, 'row', None, 'col'), may hold values from -6 to 6
Outputs:
- diagonal_factor: float32 [16, 32, 32, 16], P(None, 'row', None, 'col')
- panel_factor: bfloat16 [4, 32, 512, 512], P(None, 'row', 'col')
- updated_trailing: bfloat16 [4, 32, 512, 16, 512], P(None, 'row', None, 'col')
Inputs may be any that keep to these rules, and one draw needn't show every extreme that they name: `diagonal_tile`: symmetric positive definite: a Matern covariance of sites a few kilometres apart plus a nugget.
All inputs are finite; a program needn't handle non-finite values.
Results may differ from a plain program's by a relative error of at most 0.0053.
Values may be sent and summed in bfloat16 or wider, within the bound.
No kernel may reach another device: no remote copies, remote signals or barrier semaphores. Data moves between devices by JAX's collectives and lax.ppermute only.
A program may use at most 64 MiB of HBM per device.

v0:
```python
import jax
import jax.numpy as jnp
from jax import lax
from jax.sharding import PartitionSpec as P

NB = 512


def broadcast(block, axis, source):
    block = jnp.where(lax.axis_index(axis) == source, block, jnp.zeros_like(block))
    return lax.psum(block, axis)


def solve_rows(rows, inverse_t):
    return jnp.dot(rows.astype(jnp.float32), inverse_t, precision=lax.Precision.HIGHEST).astype(
        jnp.bfloat16
    )


def on_device(panel, diagonal_tile, trailing):
    rows_count = lax.axis_size("row")
    cols_count = lax.axis_size("col")
    row_at = lax.axis_index("row")
    col_at = lax.axis_index("col")
    piece_rows, piece_cols = diagonal_tile.shape
    band = lax.all_gather(diagonal_tile, "col", axis=1, tiled=True)
    full = lax.all_gather(band, "row", axis=0, tiled=True)
    factor = jnp.linalg.cholesky(full)
    inverse = lax.linalg.triangular_solve(
        factor, jnp.eye(NB, dtype=jnp.float32), left_side=True, lower=True
    )
    inverse_t = inverse.T
    own_strips = solve_rows(panel, inverse_t)
    solved = lax.all_gather(own_strips, "col", axis=2, tiled=True)
    column = broadcast(solved[0, 0], "row", col_at)
    product = jnp.einsum("tap,bp->tab", solved[:, 0], column, preferred_element_type=jnp.float32)
    current = trailing[:, 0, :, 0, :].astype(jnp.float32)
    updated = (current - product).astype(jnp.bfloat16)
    updated = updated.reshape(trailing.shape)
    cyclic = factor.reshape(piece_rows, rows_count, piece_cols, cols_count)
    zero = jnp.zeros((), jnp.int32)
    own_factor = lax.dynamic_slice(
        cyclic, (zero, row_at, zero, col_at), (piece_rows, 1, piece_cols, 1)
    )
    return (own_factor, own_strips, updated)


def solution(mesh):
    in_specs = (P(None, "row", "col", None), P("row", "col"), P(None, "row", None, "col", None))
    out_specs = (
        P(None, "row", None, "col"),
        P(None, "row", "col", None),
        P(None, "row", None, "col", None),
    )
    return jax.shard_map(
        on_device, mesh=mesh, in_specs=in_specs, out_specs=out_specs, check_vma=False
    )
```

profile of v0, /device:TPU:1, one launch (start us, length us, event | category | flops | bytes accessed | tf_op | source)
XLA Modules:
  0.0 470.5 jit_solution(816734454172398936)
XLA Ops:
  7.2 0.0 copy-start
  7.2 0.0 all-gather.5.cloned.1.call-start
  7.2 30.1 %all-gather.1 = f32[16,32,16]{1,2,0:T(8,128)S(1)} all-gather(f32[1,32,16]{1,2,0:T(8,128)} %bitcast.87), channel_id=1, replica_groups=mesh['row'=32,'col'=16] {'col'}, dimensions={0}, use_global_device_ids=true | all-gather | bytes 34816 | tf_op jit(solution)/shard_map/all_gather | solution.py:26
  37.4 0.7 reshape.88
  38.1 0.0 all-gather.5.cloned.1.call-update
  38.1 0.0 all-gather.7.cloned.1.call-start
  38.2 0.1 iota_compare_fusion
  38.3 0.1 fusion.20
  38.4 61.5 %all-gather.5.cloned.1.call-done = f32[512,512]{1,0:T(8,128)} async-done(((f32[16,512]{1,0:T(8,128)}), f32[512,512]{1,0:T(8,128)}) %all-gather.5.cloned.1.call-update) | async-done | bytes 1048592 | tf_op jit(solution)/shard_map/all_gather | solution.py:27
  99.9 1.6 copy.26
  101.6 0.2 fusion.8
  101.8 0.0 copy-start.2
  101.8 1.0 copy-done.2
  102.8 11.7 %cholesky.104 = f32[128,128]{1,0:T(8,128)S(1)} custom-call(f32[128,128]{1,0:T(8,128)S(1)} %cholesky.266), custom_call_target="Cholesky" | custom-call | tf_op jit(solution)/shard_map/jit(cholesky)/cholesky | solution.py:28
  114.5 0.1 cholesky.224
  114.6 9.8 %custom-call.30 = f32[1,128,128]{1,2,0:T(8,128)S(1)} custom-call(f32[1,128,128]{2,1,0:T(8,128)S(1)} %get-tuple-element.44), custom_call_target="InvertDiagBlocksLowerTriangular" | custom-call | tf_op jit(solution)/shard_map/jit(cholesky)/cholesky | solution.py:28
  124.5 1.2 constant_dynamic-update-slice_fusion.3
  125.7 1.3 convolution_subtract_fusion.3
  127.0 11.7 %cholesky.217 = f32[128,128]{1,0:T(8,128)S(1)} custom-call(f32[128,128]{1,0:T(8,128)S(1)} %cholesky.270), custom_call_target="Cholesky" | custom-call | tf_op jit(solution)/shard_map/jit(cholesky)/cholesky | solution.py:28
  138.7 10.0 %custom-call.31 = f32[1,128,128]{1,2,0:T(8,128)S(1)} custom-call(f32[1,128,128]{2,1,0:T(8,128)S(1)} %get-tuple-element.41), custom_call_target="InvertDiagBlocksLowerTriangular" | custom-call | tf_op jit(solution)/shard_map/jit(cholesky)/cholesky | solution.py:28
  148.7 0.3 convolution_dynamic-update-slice_fusion
  149.0 1.3 convolution_subtract_fusion.4
  150.3 11.7 %cholesky.238 = f32[128,128]{1,0:T(8,128)S(1)} custom-call(f32[128,128]{1,0:T(8,128)S(1)} %cholesky.275), custom_call_target="Cholesky" | custom-call | tf_op jit(solution)/shard_map/jit(cholesky)/cholesky | solution.py:28
  162.0 9.8 %custom-call.32 = f32[1,128,128]{1,2,0:T(8,128)S(1)} custom-call(f32[1,128,128]{2,1,0:T(8,128)S(1)} %get-tuple-element.38), custom_call_target="InvertDiagBlocksLowerTriangular" | custom-call | tf_op jit(solution)/shard_map/jit(cholesky)/cholesky | solution.py:28
  171.8 0.2 convolution_dynamic-update-slice_fusion.1
  172.0 1.2 convolution_subtract_fusion.5
  173.3 11.7 %cholesky.255 = f32[128,128]{1,0:T(8,128)S(1)} custom-call(f32[128,128]{1,0:T(8,128)S(1)} %convolution_subtract_fusion.5), custom_call_target="Cholesky" | custom-call | tf_op jit(solution)/shard_map/jit(cholesky)/cholesky | solution.py:28
  185.0 0.6 compare_reduce_fusion.1
  185.7 0.9 compare_reduce_fusion
  186.6 0.6 compare_reduce_fusion.2
  189.8 1.2 fusion.9
  191.1 14.0 %while.1 = (s32[]{:T(128)}, f32[512,512]{1,0:T(8,128)}, s32[4,2]{0,1:T(2,128)S(1)}, f32[4,128,128]{2,1,0:T(8,128)}, s32[]{:T(128)}) while((s32[]{:T(128)}, f32[512,512]{1,0:T(8,128)}, s32[4,2]{0,1:T(2,128)S(1)}, f32[4,128,128]{2,1,0:T(8,128)}, s32[]{:T(128)}) %tuple.36), condition=%wide.while_cond, body=%wide.while_body.sunk | while | flops 2 | bytes 132205 | solution.py:29
  191.1 0.1 constant_dynamic-slice_fusion.3
  191.1 0.5 fusion.52
  191.7 2.9 bitcast_dynamic-update-slice_fusion.2
  194.6 0.1 constant_dynamic-slice_fusion.3
  194.6 0.5 fusion.52
  195.2 2.9 bitcast_dynamic-update-slice_fusion.2
  198.1 0.1 constant_dynamic-slice_fusion.3
  198.2 0.5 fusion.52
  198.7 2.9 bitcast_dynamic-update-slice_fusion.2
  201.6 0.1 constant_dynamic-slice_fusion.3
  201.7 0.5 fusion.52
  202.2 2.8 bitcast_dynamic-update-slice_fusion.2
  205.0 40.1 %custom-call.33 = f32[4,128,128]{1,2,0:T(8,128)S(1)} custom-call(f32[4,128,128]{2,1,0:T(8,128)} %get-tuple-element.10), custom_call_target="InvertDiagBlocksLowerTriangular" | custom-call | tf_op jit(solution)/shard_map/triangular_solve | solution.py:29
  245.2 0.3 fusion.22
  245.5 1.2 convolution_subtract_fusion.1
  246.7 0.4 fusion.35
  247.1 1.3 convolution_subtract_fusion
  248.5 0.4 fusion.33
  248.9 1.6 convolution_subtract_fusion.2
  250.5 0.4 fusion.32
  250.9 1.4 convolution_convert_fusion
  252.3 0.0 all-gather.7.cloned.1.call-update
  252.3 0.0 all-reduce.3.cloned.1.call-start
  252.4 63.1 %all-gather.7.cloned.1.call-done = bf16[4,512,512]{2,1,0:T(8,128)(2,1)} async-done(((bf16[4,32,512]{2,1,0:T(8,128)(2,1)}), bf16[4,512,512]{2,1,0:T(8,128)(2,1)}) %all-gather.7.cloned.1.call-update) | async-done | bytes 2097168 | tf_op jit(solution)/shard_map/all_gather | solution.py:34
  315.5 1.9 fusion.15
  317.4 0.0 all-reduce.3.cloned.1.call-update
  317.4 0.3 copy.27
  317.8 2.5 reshape.57
  320.2 1.1 constant_dynamic-slice_fusion.1
  321.3 0.8 copy.29
  322.1 137.4 %all-reduce.3.cloned.1.call-done = bf16[512,512]{1,0:T(8,128)(2,1)} async-done(((bf16[512,512]{1,0:T(8,128)(2,1)}), bf16[512,512]{1,0:T(8,128)(2,1)}) %all-reduce.3.cloned.1.call-update) | async-done | bytes 524304 | tf_op jit(solution)/shard_map/psum | solution.py:11
  459.6 4.4 fusion.1
  (16 shorter events, 0.2 us)
Async XLA Ops:
  7.2 243.7 %copy-start = (bf16[4,1,32,512]{3,2,1,0:T(8,128)(2,1)S(1)}, bf16[4,1,32,512]{3,2,1,0:T(8,128)(2,1)}, u32[]{:S(2)}) copy-start(bf16[4,1,32,512]{3,2,1,0:T(8,128)(2,1)} %param.3) | copy-start | bytes 393220
  7.2 92.7 %all-gather.5.cloned.1.call-start = ((), (), s32[]{:S(2)}) async-start(), calls=%async_computation | async-start | bytes 1081344 | tf_op jit(solution)/shard_map/all_gather | solution.py:27
  38.1 277.4 %all-gather.7.cloned.1.call-start = ((), (), s32[]{:S(2)}) async-start(), calls=%async_computation.2 | async-start | bytes 2228224 | tf_op jit(solution)/shard_map/all_gather | solution.py:34
  99.9 1.7 copy-start.1
  101.8 1.0 copy-start.2
  252.3 207.3 %all-reduce.3.cloned.1.call-start = ((), (), s32[]{:S(2)}) async-start(), calls=%async_computation.1 | async-start | bytes 1048576 | tf_op jit(solution)/shard_map/psum | solution.py:11
  317.7 141.8 %copy-start.3 = (bf16[4,512,512]{2,1,0:T(8,128)(2,1)S(1)}, bf16[4,512,512]{2,1,0:T(8,128)(2,1)}, u32[]{:S(2)}) copy-start(bf16[4,512,512]{2,1,0:T(8,128)(2,1)} %all-gather.7.cloned.1.call-done) | copy-start | bytes 6291460
Sparse Core Ops, SparseCore 0:
  38.2 61.6 all-gather.4
  252.4 63.0 all-gather.6
  319.3 140.2 all-reduce.2
where the time goes:
time: 471 us; the launch traced here: 470 us
  waiting for transfers between devices  262 us (56%)
  other arithmetic  122 us (26%)
  blocking collectives  30.1 us (6%)
  local copies, waits for them, and re-layouts  22.2 us (5%)
  matrix products  16.9 us (4%)
  between operations  16.7 us (4%)
    psum x1, waiting for transfers between devices, broadcast(): return lax.psum(block, axis)  137 us
    another operation x14, other arithmetic, on_device(): factor = jnp.linalg.cholesky(full)  78.7 us
    all_gather x1, waiting for transfers between devices, on_device(): solved = lax.all_gather(own_strips, 'col', axis=2, tiled=True)  63.1 us
    all_gather x1, waiting for transfers between devices, on_device(): full = lax.all_gather(band, 'row', axis=0, tiled=True)  61.5 us
    another operation x3, other arithmetic, on_device(): lax.linalg.triangular_solve(factor, jnp.eye(NB, dtype=jnp.float32), left_...  41.4 us
    all_gather x1, blocking collectives, on_device(): band = lax.all_gather(diagonal_tile, 'col', axis=1, tiled=True)  30.1 us
    another operation x12, local copies, waits for them, and re-layouts  14 us
  transfers between devices with their start and end apart: 3, of which 3 were waited for; matrix products, arithmetic and copies ran while one was open for 1% of the time, Pallas kernels for 0%

commit v1 on v0

v1 whole, which is shorter than its diff:
```python
import jax
import jax.numpy as jnp
from jax import lax
from jax.experimental import pallas as pl
from jax.experimental.pallas import tpu as pltpu
from jax.sharding import PartitionSpec as P

NB = 512
BLOCK = 128
F32, BF16 = jnp.float32, jnp.bfloat16
NT = (((1,), (1,)), ((), ()))
NN = (((1,), (0,)), ((), ()))


def split(x):
    high = x.astype(BF16)
    return high, (x - high.astype(F32)).astype(BF16)


def dot(a, b, dims):
    return lax.dot_general(a, b, dims, preferred_element_type=F32)


def dot_split(a, b, dims):
    a_high, a_low = split(a)
    b_high, b_low = split(b)
    return dot(a_high, b_high, dims) + (dot(a_high, b_low, dims) + dot(a_low, b_high, dims))


def over_lanes(x, j):
    return jnp.broadcast_to(x[:, j : j + 1], x.shape)


def over_rows(x, k):
    return jnp.broadcast_to(x[k : k + 1, :], x.shape)


def factor_block(block):
    row = lax.broadcasted_iota(jnp.int32, (8, BLOCK), 0)
    lane = lax.broadcasted_iota(jnp.int32, (8, BLOCK), 1)
    count = BLOCK // 8
    left = [block[8 * i : 8 * i + 8, :] for i in range(count)]
    right = [jnp.where(lane == row + 8 * i, 1.0, 0.0).astype(F32) for i in range(count)]
    upper, inverse = [], []
    for b in range(count):
        cols = {i: [over_lanes(left[i], 8 * b + j) for j in range(8)] for i in range(b, count)}
        own = cols[b]
        pivots = jnp.ones((8, BLOCK), F32)
        for k in range(8):
            pivot = over_rows(own[k], k)
            recip = 1.0 / pivot
            pivots = jnp.where(row == k, pivot, pivots)
            entries = {j: over_rows(own[j], k) for j in range(k + 1, 8)}
            mult = jnp.where(row > k, own[k] * recip, 0.0)
            left_row, right_row = over_rows(left[b], k), over_rows(right[b], k)
            left[b] = left[b] - mult * left_row
            right[b] = right[b] - mult * right_row
            for j in range(k + 1, 8):
                own[j] = own[j] - mult * entries[j]
            for i in range(b + 1, count):
                below = cols[i]
                mult = below[k] * recip
                for j in range(k + 1, 8):
                    below[j] = below[j] - mult * entries[j]
                left[i] = left[i] - mult * left_row
                right[i] = right[i] - mult * right_row
        scale = lax.rsqrt(pivots)
        upper.append(jnp.where(lane >= row + 8 * b, left[b] * scale, 0.0))
        inverse.append(right[b] * scale)
    return jnp.concatenate(upper, 0), jnp.concatenate(inverse, 0)


def factor_kernel(at_ref, tile_ref, own_ref, high_ref, low_ref, work, factor, inverse):
    work[...] = tile_ref[...]
    factor[...] = jnp.zeros_like(factor)
    inverse[...] = jnp.zeros_like(inverse)
    for start in range(0, NB, BLOCK):
        here = pl.ds(start, BLOCK)
        before = pl.ds(0, start)
        upto = pl.ds(0, start + BLOCK)
        after = pl.ds(start + BLOCK, NB - start - BLOCK)
        upper, block_inverse = factor_block(work[here, here])
        factor[here, here] = upper.T
        inverse[here, here] = block_inverse
        if start:
            inverse[here, before] = dot_split(block_inverse, inverse[here, before], NN)
        if start + BLOCK < NB:
            below = dot_split(work[after, here], block_inverse, NT)
            factor[after, here] = below
            work[after, after] = work[after, after] - dot_split(below, below, NT)
            inverse[after, upto] = inverse[after, upto] - dot_split(below, inverse[here, upto], NN)
    high, low = split(inverse[...])
    high_ref[...] = high
    low_ref[...] = low
    count_a, count_b = own_ref.shape
    step = NB // count_a
    rows = jnp.concatenate([factor[pl.ds(a * step + at_ref[0], 1), :] for a in range(count_a)], 0)
    source = lax.broadcasted_iota(jnp.int32, (NB, BLOCK), 0)
    target = lax.broadcasted_iota(jnp.int32, (NB, BLOCK), 1)
    pick = jnp.where(source == target * (NB // count_b) + at_ref[1], 1.0, 0.0).astype(BF16)
    first, rest = split(rows)
    second, third = split(rows - first.astype(F32))
    picked = dot(first, pick, NN) + (dot(second, pick, NN) + dot(third, pick, NN))
    own_ref[...] = picked[:, :count_b]


def update_kernel(at_ref, high_ref, low_ref, column_ref, panel_ref, trailing_ref, own_ref, out_ref, column, solved):
    high, low = high_ref[...], low_ref[...]

    @pl.when(pl.program_id(0) == 0)
    def _():
        tile = column_ref[...].astype(BF16)
        column[...] = (dot(tile, high, NT) + dot(tile, low, NT)).astype(BF16)

    rows = panel_ref[...].reshape(NB, NB)
    result = (dot(rows, high, NT) + dot(rows, low, NT)).astype(BF16)
    solved[...] = result
    strip = own_ref.shape[1]
    own_ref[0] = solved[pl.ds(pl.multiple_of(at_ref[1] * strip, strip), strip), :]
    product = dot(result, column[...], NT)
    out_ref[0] = (trailing_ref[0].astype(F32) - product).astype(BF16)


def to_all(x, axis):
    count = lax.axis_size(axis)
    return lax.all_to_all(jnp.broadcast_to(x[None], (count,) + x.shape), axis, 0, 0)


def on_device(panel, diagonal_tile, trailing):
    rows_count = lax.axis_size("row")
    cols_count = lax.axis_size("col")
    tiles = panel.shape[0]
    strip = panel.shape[2]
    half = NB // rows_count
    at = jnp.stack([lax.axis_index("row"), lax.axis_index("col")]).astype(jnp.int32)
    panel = panel.reshape(tiles, strip, NB)
    trailing = trailing.reshape(tiles, NB, NB)

    gathered = lax.all_gather(panel, "col")

    piece = jnp.zeros((half, NB), F32)
    for h in range(2):
        pairs = [
            (c * cols_count + s, (2 * s + h) * cols_count + c)
            for c in range(cols_count)
            for s in range(cols_count)
        ]
        piece = piece + lax.ppermute(panel[0, h * half : (h + 1) * half], ("row", "col"), pairs).astype(F32)

    pieces = to_all(diagonal_tile, "col")
    band = pieces.transpose(1, 0, 2).reshape(-1, NB)
    tile = to_all(band, "row").reshape(NB, NB)
    column = to_all(piece, "row").reshape(NB, NB)

    params = pltpu.CompilerParams(vmem_limit_bytes=48 << 20)
    smem = pl.BlockSpec(memory_space=pltpu.SMEM)
    own_factor, high, low = pl.pallas_call(
        factor_kernel,
        in_specs=[smem, pl.BlockSpec(memory_space=pltpu.VMEM)],
        out_shape=[
            jax.ShapeDtypeStruct((NB // rows_count, NB // cols_count), F32),
            jax.ShapeDtypeStruct((NB, NB), BF16),
            jax.ShapeDtypeStruct((NB, NB), BF16),
        ],
        scratch_shapes=[pltpu.VMEM((NB, NB), F32)] * 3,
        compiler_params=params,
        cost_estimate=pl.CostEstimate(flops=12 * NB**3, bytes_accessed=3 << 20, transcendentals=0),
    )(at, tile)

    whole = pl.BlockSpec((NB, NB), lambda t: (0, 0))
    own_strips, updated = pl.pallas_call(
        update_kernel,
        grid=(tiles,),
        in_specs=[
            smem,
            whole,
            whole,
            whole,
            pl.BlockSpec((cols_count, 1, strip, NB), lambda t: (0, t, 0, 0)),
            pl.BlockSpec((1, NB, NB), lambda t: (t, 0, 0)),
        ],
        out_specs=[
            pl.BlockSpec((1, strip, NB), lambda t: (t, 0, 0)),
            pl.BlockSpec((1, NB, NB), lambda t: (t, 0, 0)),
        ],
        out_shape=[
            jax.ShapeDtypeStruct((tiles, strip, NB), BF16),
            jax.ShapeDtypeStruct((tiles, NB, NB), BF16),
        ],
        scratch_shapes=[pltpu.VMEM((NB, NB), BF16)] * 2,
        compiler_params=params,
        cost_estimate=pl.CostEstimate(flops=30 * NB**3, bytes_accessed=8 << 20, transcendentals=0),
    )(at, high, low, column, gathered, trailing)

    return (
        own_factor.reshape(NB // rows_count, 1, NB // cols_count, 1),
        own_strips.reshape(tiles, 1, strip, NB),
        updated.reshape(tiles, 1, NB, 1, NB),
    )


def solution(mesh):
    in_specs = (P(None, "row", "col", None), P("row", "col"), P(None, "row", None, "col", None))
    out_specs = (
        P(None, "row", None, "col"),
        P(None, "row", "col", None),
        P(None, "row", None, "col", None),
    )
    return jax.shard_map(
        on_device, mesh=mesh, in_specs=in_specs, out_specs=out_specs, check_vma=False
    )
```

time: 471 us -> 111 us (0.24)
  waiting for transfers between devices: 262 us -> 11 us
  other arithmetic: 122 us -> 0.8 us
  Pallas kernels: 0 us -> 26.9 us
  starting transfers between devices: 0.12 us -> 24.7 us
  matrix products: 16.9 us -> 0 us
  local copies, waits for them, and re-layouts: 22.2 us -> 6.1 us
    psum x1 -> x0, waiting for transfers between devices: 137 us -> none  [broadcast(): return lax.psum(block, axis)]
    all_gather x2 -> x1, waiting for transfers between devices: 125 us -> 0.01 us  [on_device(): gathered = lax.all_gather(panel, 'col')]
    another operation x17 -> x1, other arithmetic: 120 us -> 0.08 us  [on_device(): jnp.stack([lax.axis_index('row'), lax.axis_index('col')]).astype(jnp.int32)]
    all_gather x1 -> x0, blocking collectives: 30.1 us -> none  [on_device(): band = lax.all_gather(diagonal_tile, 'col', axis=1, tiled=True)]
    all_to_all x0 -> x1, blocking collectives: none -> 27 us  [to_all(): lax.all_to_all(jnp.broadcast_to(x[None], (count,) + x.shape), axis, 0, 0)]
    pallas_call x0 -> x2, Pallas kernels: none -> 26.9 us  [the longest x1 19.7 us: on_device(): pl.pallas_call(factor_kernel, in_specs=[smem, pl.BlockSpec(memory_space=p...]
    all_to_all x0 -> x2, starting transfers between devices: none -> 18.8 us  [to_all(): lax.all_to_all(jnp.broadcast_to(x[None], (count,) + x.shape), axis, 0, 0)]
    another operation x17 -> x0, local copies, waits for them, and re-layouts: 14.1 us -> none
  transfers between devices with their start and end apart: 3 -> 5, of which waited for: 3 -> 2; matrix products, arithmetic and copies ran while one was open for 1% -> 5% of each run, Pallas kernels for 0% -> 18%
where the time goes in v1:
time: 111 us
  blocking collectives  27 us (24%)
  Pallas kernels  26.9 us (24%)
  starting transfers between devices  24.7 us (22%)
  between operations  14.1 us (13%)
  waiting for transfers between devices  11 us (10%)
  local copies, waits for them, and re-layouts  6.1 us (5%)
    all_to_all x1, blocking collectives, to_all(): lax.all_to_all(jnp.broadcast_to(x[None], (count,) + x.shape), axis, 0, 0)  27 us
    pallas_call x1, Pallas kernels, on_device(): pl.pallas_call(factor_kernel, in_specs=[smem, pl.BlockSpec(memory_space=p...  19.7 us
    all_to_all x2, starting transfers between devices, to_all(): lax.all_to_all(jnp.broadcast_to(x[None], (count,) + x.shape), axis, 0, 0)  18.8 us
    all_to_all x2, waiting for transfers between devices, to_all(): lax.all_to_all(jnp.broadcast_to(x[None], (count,) + x.shape), axis, 0, 0)  9.44 us
    pallas_call x1, Pallas kernels, on_device(): pl.pallas_call(update_kernel, grid=(tiles,), in_specs=[smem, whole, whole...  7.2 us
    ppermute x2, starting transfers between devices, on_device(): lax.ppermute(panel[0, h * half:(h + 1) * half], ('row', 'col'), pairs)  5.87 us
    broadcast_in_dim x4, local copies, waits for them, and re-layouts, to_all(): jnp.broadcast_to(x[None], (count,) + x.shape)  3.01 us
  transfers between devices with their start and end apart: 5, of which 2 were waited for; matrix products, arithmetic and copies ran while one was open for 5% of the time, Pallas kernels for 18%

profile of v1, /device:TPU:1, one launch (start us, length us, event | category | flops | bytes accessed | tf_op | source)
XLA Modules:
  0.0 110.6 jit_solution(6081560503437607260)
XLA Ops:
  7.2 0.0 all-gather.3.cloned.1.call-start
  7.2 0.7 all-gather.3.cloned.1.call-update
  7.9 0.7 broadcast_in_dim.8
  8.6 0.1 reshape.38
  8.7 27.0 %all_to_all.15 = f32[16,1,512]{2,1,0:T(1,128)S(1)} all-to-all(f32[16,1,512]{2,1,0:T(1,128)S(1)} %reshape.38), channel_id=1, replica_groups=mesh['row'=32,'col'=16] {'col'}, dimensions={0} | all-to-all | bytes 65536 | tf_op jit(solution)/shard_map/all_to_all | solution.py:126
  35.7 0.5 broadcast.2
  36.3 0.7 reduce
  37.0 0.1 reshape.39
  37.1 0.1 broadcast_in_dim.9
  37.2 1.1 broadcast_in_dim.10
  38.3 9.2 %all-to-all-start.1 = ((f32[32,16,512]{2,1,0:T(8,128)}), f32[32,16,512]{2,1,0:T(8,128)S(1)}, u32[]{:S(2)}, u32[]{:S(2)}) async-start(f32[32,16,512]{2,1,0:T(8,128)} %broadcast_in_dim.10), calls=%async_computation.1 | async-start | bytes 2097152 | tf_op jit(solution)/shard_map/all_to_all | solution.py:126
  47.6 0.7 slice_bitcast_fusion.1
  48.3 2.4 %collective-permute-start = (bf16[16,512]{1,0:T(8,128)(2,1)S(1)}, bf16[16,512]{1,0:T(8,128)(2,1)S(1)}, u32[]{:S(2)}, u32[]{:S(2)}) collective-permute-start(bf16[16,512]{1,0:T(8,128)(2,1)S(1)} %get-tuple-element.22), channel_id=1, source_target_pairs={{0,0},{1,32},{2,64},{3,96},{4,128},{5,160},{6,192},{7,224},{8,256}... | collective-permute-start | bytes 49160 | tf_op jit(solution)/shard_map/ppermute | solution.py:148
  50.8 3.4 %collective-permute-start.1 = (bf16[16,512]{1,0:T(8,128)(2,1)S(1)}, bf16[16,512]{1,0:T(8,128)(2,1)S(1)}, u32[]{:S(2)}, u32[]{:S(2)}) collective-permute-start(bf16[16,512]{1,0:T(8,128)(2,1)S(1)} %get-tuple-element.23), channel_id=1, source_target_pairs={{0,16},{1,48},{2,80},{3,112},{4,144},{5,176},{6,208},{7,240},{8,27... | collective-permute-start | bytes 49160 | tf_op jit(solution)/shard_map/ppermute | solution.py:148
  54.2 0.0 collective-permute-done
  54.2 0.8 collective-permute-done.1
  55.1 9.4 %all-to-all-done.1 = f32[32,16,512]{2,1,0:T(8,128)S(1)} async-done(((f32[32,16,512]{2,1,0:T(8,128)}), f32[32,16,512]{2,1,0:T(8,128)S(1)}, u32[]{:S(2)}, u32[]{:S(2)}) %all-to-all-start.1) | async-done | bytes 1048608 | tf_op jit(solution)/shard_map/all_to_all | solution.py:126
  64.5 1.1 broadcast_in_dim.22
  65.6 9.6 %all-to-all-start.2 = ((f32[32,16,512]{2,1,0:T(8,128)}), f32[32,16,512]{2,1,0:T(8,128)S(1)}, u32[]{:S(2)}, u32[]{:S(2)}) async-start(f32[32,16,512]{2,1,0:T(8,128)} %broadcast_in_dim.22), calls=%async_computation.2 | async-start | bytes 2097152 | tf_op jit(solution)/shard_map/all_to_all | solution.py:126
  75.2 0.1 pad_add_fusion.at_ref
  75.3 19.7 %shard_map.58 = (f32[16,32]{1,0:T(8,128)}, bf16[512,512]{1,0:T(8,128)(2,1)S(1)}, bf16[512,512]{1,0:T(8,128)(2,1)S(1)}) custom-call(s32[2]{0:T(128)S(1)} %pad_add_fusion.at_ref, f32[512,512]{1,0:T(8,128)S(1)} %bitcast.21), custom_call_target="tpu_custom_call" | custom-call | flops 1610612736 | bytes 3145728 | tf_op jit(solution)/shard_map/pallas_call | solution.py:157
  95.0 0.0 all-to-all-done.2
  95.0 0.0 all-gather.3.cloned.1.call-done
  95.0 0.0 copy-start
  95.0 1.6 %copy-done = bf16[64,1,32,512]{3,2,1,0:T(8,128)(2,1)S(1)} copy-done((bf16[64,1,32,512]{3,2,1,0:T(8,128)(2,1)S(1)}, bf16[64,1,32,512]{3,2,1,0:T(8,128)(2,1)}, u32[]{:S(2)}) %copy-start) | copy-done | bytes 2097176
  96.6 7.2 %shard_map.59 = (bf16[4,32,512]{2,1,0:T(8,128)(2,1)}, bf16[4,512,512]{2,1,0:T(8,128)(2,1)}) custom-call(s32[2]{0:T(128)S(1)} %pad_add_fusion.at_ref, bf16[512,512]{1,0:T(8,128)(2,1)S(1)} %get-tuple-element.9.high_ref, bf16[512,512]{1,0:T(8,128)(2,1)S(1)} %get-tuple-element.10.low_ref, f32[512,512]{1,0:T(8,128)S(1)} %bitcast.22, ...), custom_call_target="tpu_custom_call" | custom-call | flops 4026531840 | bytes 8388608 | tf_op jit(solution)/shard_map/pallas_call | solution.py:171
  (2 shorter events, 0.1 us)
Async XLA Ops:
  7.2 87.8 %all-gather.3.cloned.1.call-start = ((), (), s32[]{:S(2)}) async-start(), calls=%async_computation.3 | async-start | bytes 2228224 | tf_op jit(solution)/shard_map/all_gather | solution.py:139
  38.3 26.2 %all-to-all-start.1 = ((f32[32,16,512]{2,1,0:T(8,128)}), f32[32,16,512]{2,1,0:T(8,128)S(1)}, u32[]{:S(2)}, u32[]{:S(2)}) async-start(f32[32,16,512]{2,1,0:T(8,128)} %broadcast_in_dim.10), calls=%async_computation.1 | async-start | bytes 2097152 | tf_op jit(solution)/shard_map/all_to_all | solution.py:126
  48.3 5.9 %collective-permute-start = (bf16[16,512]{1,0:T(8,128)(2,1)S(1)}, bf16[16,512]{1,0:T(8,128)(2,1)S(1)}, u32[]{:S(2)}, u32[]{:S(2)}) collective-permute-start(bf16[16,512]{1,0:T(8,128)(2,1)S(1)} %get-tuple-element.22), channel_id=1, source_target_pairs={{0,0},{1,32},{2,64},{3,96},{4,128},{5,160},{6,192},{7,224},{8,256}... | collective-permute-start | bytes 49160 | tf_op jit(solution)/shard_map/ppermute | solution.py:148
  50.8 4.3 %collective-permute-start.1 = (bf16[16,512]{1,0:T(8,128)(2,1)S(1)}, bf16[16,512]{1,0:T(8,128)(2,1)S(1)}, u32[]{:S(2)}, u32[]{:S(2)}) collective-permute-start(bf16[16,512]{1,0:T(8,128)(2,1)S(1)} %get-tuple-element.23), channel_id=1, source_target_pairs={{0,16},{1,48},{2,80},{3,112},{4,144},{5,176},{6,208},{7,240},{8,27... | collective-permute-start | bytes 49160 | tf_op jit(solution)/shard_map/ppermute | solution.py:148
  65.6 29.4 %all-to-all-start.2 = ((f32[32,16,512]{2,1,0:T(8,128)}), f32[32,16,512]{2,1,0:T(8,128)S(1)}, u32[]{:S(2)}, u32[]{:S(2)}) async-start(f32[32,16,512]{2,1,0:T(8,128)} %broadcast_in_dim.22), calls=%async_computation.2 | async-start | bytes 2097152 | tf_op jit(solution)/shard_map/all_to_all | solution.py:126
  95.0 1.6 %copy-start = (bf16[64,1,32,512]{3,2,1,0:T(8,128)(2,1)S(1)}, bf16[64,1,32,512]{3,2,1,0:T(8,128)(2,1)}, u32[]{:S(2)}) copy-start(bf16[64,1,32,512]{3,2,1,0:T(8,128)(2,1)} %all-gather.3.cloned.1.call-done) | copy-start | bytes 6291460
Sparse Core Ops, SparseCore 0:
  10.1 71.5 all-gather.2

commit v2 on v1

v2 whole, which is shorter than its diff:
```python
import jax
import jax.numpy as jnp
from jax import lax
from jax.experimental import pallas as pl
from jax.experimental.pallas import tpu as pltpu
from jax.sharding import PartitionSpec as P

NB = 512
BLOCK = 128
LANES = 128
F32, BF16 = jnp.float32, jnp.bfloat16
NT = (((1,), (1,)), ((), ()))
NN = (((1,), (0,)), ((), ()))


def split(x):
    high = x.astype(BF16)
    return high, (x - high.astype(F32)).astype(BF16)


def dot(a, b, dims):
    return lax.dot_general(a, b, dims, preferred_element_type=F32)


def dot_split(a, b, dims):
    a_high, a_low = split(a)
    b_high, b_low = split(b)
    return dot(a_high, b_high, dims) + (dot(a_high, b_low, dims) + dot(a_low, b_high, dims))


def over_lanes(x, j):
    return jnp.broadcast_to(x[:, j : j + 1], x.shape)


def over_rows(x, k):
    return jnp.broadcast_to(x[k : k + 1, :], x.shape)


def total(terms):
    while len(terms) > 1:
        terms = [sum(terms[i : i + 2]) for i in range(0, len(terms), 2)]
    return terms[0]


def factor_block(block):
    row = lax.broadcasted_iota(jnp.int32, (8, BLOCK), 0)
    lane = lax.broadcasted_iota(jnp.int32, (8, BLOCK), 1)
    count = BLOCK // 8
    work = [block[8 * i : 8 * i + 8, :] for i in range(count)]
    upper, inverse = [], []

    def spread_columns(i, b):
        return [over_lanes(work[i], 8 * b + j) for j in range(8)]

    def eliminate(i, b, weights, columns):
        inside = (lane >= 8 * b) & (lane < 8 * b + 8)
        terms = [columns[k] * weights[k] for k in range(8)]
        work[i] = jnp.where(inside, 0.0, work[i]) - total(terms)

    weights = None
    for b in range(count):
        inside = (lane >= 8 * b) & (lane < 8 * b + 8)
        own = spread_columns(b, b)
        if b:
            for i in range(b + 1, count):
                eliminate(i, b - 1, weights, spread_columns(i, b - 1))
        if b + 1 < count:
            following = spread_columns(b + 1, b)
        identity = jnp.where(lane == row + 8 * b, 1.0, 0.0).astype(F32)
        left = work[b]
        right = rows = jnp.where(inside, identity, work[b])
        scale = jnp.zeros((8, BLOCK), F32)
        cross = jnp.zeros((8, BLOCK), F32)
        for k in range(0, 8, 2):
            first, second = row == k, row == k + 1
            pair = first | second
            head, off, tail = over_rows(own[k], k), over_rows(own[k + 1], k), over_rows(own[k + 1], k + 1)
            det = head * tail - off * off
            recip = 1.0 / det
            lead = own[k] * tail - own[k + 1] * off
            trail = own[k + 1] * head - own[k] * off
            lead_all = jnp.where(first, -tail, jnp.where(second, off, lead))
            trail_all = jnp.where(first, off, jnp.where(second, -head, trail))
            for j in range(8):
                if j not in (k, k + 1):
                    change = lead_all * over_rows(own[j], k) + trail_all * over_rows(own[j], k + 1)
                    own[j] = jnp.where(pair, 0.0, own[j]) - recip * change
            own[k], own[k + 1] = -(recip * lead_all), -(recip * trail_all)
            if k < 6:
                lead = jnp.where(row > k + 1, lead, 0.0)
                trail = jnp.where(row > k + 1, trail, 0.0)
                left = left - recip * (lead * over_rows(left, k) + trail * over_rows(left, k + 1))
                right = right - recip * (lead * over_rows(right, k) + trail * over_rows(right, k + 1))
            root, root_det = lax.rsqrt(head), lax.rsqrt(det)
            scale = jnp.where(first, root, jnp.where(second, root_det * (head * root), scale))
            cross = jnp.where(second, -(off * root * root_det), cross)
        solved = total([own[j] * over_rows(rows, j) for j in range(8)])
        weights = [over_rows(solved, k) for k in range(8)]
        if b + 1 < count:
            eliminate(b + 1, b, weights, following)
        left = left * scale + pltpu.roll(left, 1, 0) * cross
        right = right * scale + pltpu.roll(right, 1, 0) * cross
        upper.append(jnp.where(lane >= row + 8 * b, left, 0.0))
        inverse.append(jnp.where(lane < 8 * b + 8, right, 0.0))
    return jnp.concatenate(upper, 0), jnp.concatenate(inverse, 0)


def solve(rows, high, low):
    return (dot(rows, high, NT) + dot(rows, low, NT)).astype(BF16)


def fold_kernel(at_ref, band_ref, out_ref):
    half = out_ref.shape[1]
    turned = pltpu.roll(band_ref[...], lax.rem(NB - at_ref[0] * half, NB), 1)
    high, low = split(turned)
    window = NB // 2
    lane = lax.broadcasted_iota(jnp.int32, (half, LANES), 1)
    high_end = high[:, window : window + LANES].astype(F32)
    low_end = pltpu.roll(low[:, window : window + LANES].astype(F32), half, 1)
    end = jnp.where(lane < half, high_end, jnp.where(lane < 2 * half, low_end, 0.0)).astype(BF16)
    block = jnp.concatenate([high[:, :window], low[:, :window], end], 1)
    for i in range(out_ref.shape[0]):
        out_ref[i] = block


def unfold(spread_ref, work, folded):
    count, half, _ = spread_ref.shape
    window = NB // 2
    lane = lax.broadcasted_iota(jnp.int32, (half, LANES), 1)
    for r in range(count):
        part = spread_ref[r].astype(F32)
        end = part[:, NB:]
        end = jnp.where(lane < half, end + pltpu.roll(end, LANES - half, 1), 0.0)
        line = jnp.concatenate([part[:, :window] + part[:, window:NB], end, jnp.zeros_like(end)], 1)
        folded[half * r : half * (r + 1), :] = pltpu.roll(line, half * r, 1) if r else line
    per_block = BLOCK // half
    row = lax.broadcasted_iota(jnp.int32, (BLOCK, BLOCK), 0) // half
    col = lax.broadcasted_iota(jnp.int32, (BLOCK, BLOCK), 1) // half
    for i in range(NB // BLOCK):
        for j in range(i + 1):
            here, there = pl.ds(BLOCK * i, BLOCK), pl.ds(BLOCK * j, BLOCK)
            gap = (i - j) * per_block
            if gap - per_block + 1 >= count // 2:
                work[here, there] = folded[here, there]
                continue
            block = folded[there, here].T
            if i == j:
                block = jnp.where(col >= row, folded[here, there], block)
            elif gap + per_block - 1 >= count // 2:
                block = jnp.where(row - col + gap >= count // 2, folded[here, there], block)
            work[here, there] = block


def factor_kernel(at_ref, spread_ref, own_ref, high_ref, low_ref, work, factor, inverse):
    unfold(spread_ref, work, factor)
    factor[...] = jnp.zeros_like(factor)
    inverse[...] = jnp.zeros_like(inverse)
    for start in range(0, NB, BLOCK):
        here = pl.ds(start, BLOCK)
        before = pl.ds(0, start)
        upto = pl.ds(0, start + BLOCK)
        after = pl.ds(start + BLOCK, NB - start - BLOCK)
        upper, block_inverse = factor_block(work[here, here])
        factor[here, here] = upper.T
        inverse[here, here] = block_inverse
        if start:
            inverse[here, before] = dot_split(block_inverse, inverse[here, before], NN)
        if start + BLOCK < NB:
            below = dot_split(work[after, here], block_inverse, NT)
            factor[after, here] = below
            work[after, after] = work[after, after] - dot_split(below, below, NT)
            inverse[after, upto] = inverse[after, upto] - dot_split(below, inverse[here, upto], NN)
    high, low = split(inverse[...])
    high_ref[...] = high
    low_ref[...] = low
    count_a, count_b = own_ref.shape
    step = NB // count_a
    rows = jnp.concatenate([factor[pl.ds(a * step + at_ref[0], 1), :] for a in range(count_a)], 0)
    source = lax.broadcasted_iota(jnp.int32, (NB, BLOCK), 0)
    target = lax.broadcasted_iota(jnp.int32, (NB, BLOCK), 1)
    pick = jnp.where(source == target * (NB // count_b) + at_ref[1], 1.0, 0.0).astype(BF16)
    first, rest = split(rows)
    second, third = split(rows - first.astype(F32))
    picked = dot(first, pick, NN) + (dot(second, pick, NN) + dot(third, pick, NN))
    own_ref[...] = picked[:, :count_b]


def update_kernel(at_ref, high_ref, low_ref, tile_ref, panel_ref, trailing_ref, own_ref, out_ref, column, solved):
    high, low = high_ref[...], low_ref[...]

    strip = own_ref.shape[1]

    @pl.when(pl.program_id(0) == 0)
    def _():
        column[...] = solve(tile_ref[: NB // strip].reshape(NB, NB), high, low)

    rows = solve(panel_ref[...].reshape(NB, NB), high, low)
    solved[...] = rows
    own_ref[0] = solved[pl.ds(pl.multiple_of(at_ref[1] * strip, strip), strip), :]
    out_ref[0] = (trailing_ref[0].astype(F32) - dot(rows, column[...], NT)).astype(BF16)


def on_device(panel, diagonal_tile, trailing):
    rows_count = lax.axis_size("row")
    cols_count = lax.axis_size("col")
    tiles = panel.shape[0]
    strip = panel.shape[2]
    half = NB // rows_count
    at = jnp.stack([lax.axis_index("row"), lax.axis_index("col")]).astype(jnp.int32)
    panel = panel.reshape(tiles, strip, NB)
    trailing = trailing.reshape(tiles, NB, NB)

    gathered = lax.all_gather(panel, "col")

    pairs = [(c * cols_count + s, s * cols_count + c) for c in range(cols_count) for s in range(cols_count)]
    piece = lax.ppermute(panel[0], ("row", "col"), pairs)

    piece_rows, piece_cols = diagonal_tile.shape
    own = diagonal_tile.reshape(-1, LANES)
    pieces = lax.all_to_all(jnp.broadcast_to(own[None], (cols_count,) + own.shape), "col", 0, 0)
    band = pieces.reshape(cols_count, piece_rows, piece_cols).transpose(1, 0, 2).reshape(-1, NB)
    vmem = pl.BlockSpec(memory_space=pltpu.VMEM)
    smem = pl.BlockSpec(memory_space=pltpu.SMEM)
    folded = pl.pallas_call(
        fold_kernel,
        in_specs=[smem, vmem],
        out_specs=vmem,
        out_shape=jax.ShapeDtypeStruct((rows_count, half, NB + LANES), BF16),
    )(at, band)
    spread = lax.all_to_all(folded, "row", 0, 0)
    piece = lax.optimization_barrier((piece, spread))[0]
    tile = lax.all_to_all(jnp.broadcast_to(piece[None], (rows_count,) + piece.shape), "row", 0, 0)

    params = pltpu.CompilerParams(vmem_limit_bytes=32 << 20)
    own_factor, high, low = pl.pallas_call(
        factor_kernel,
        grid=(1,),
        in_specs=[smem, pl.BlockSpec(spread.shape, lambda i: (0, 0, 0))],
        out_specs=[pl.BlockSpec((NB // rows_count, NB // cols_count), lambda i: (0, 0))]
        + [pl.BlockSpec((NB, NB), lambda i: (0, 0))] * 2,
        out_shape=[
            jax.ShapeDtypeStruct((NB // rows_count, NB // cols_count), F32),
        ]
        + [jax.ShapeDtypeStruct((NB, NB), BF16)] * 2,
        scratch_shapes=[pltpu.VMEM((NB, NB), F32)] * 3,
        compiler_params=params,
        cost_estimate=pl.CostEstimate(flops=12 * NB**3, bytes_accessed=3 << 20, transcendentals=0),
    )(at, spread)

    gathered = pltpu.with_memory_space_constraint(gathered, pltpu.HBM)
    trailing = pltpu.with_memory_space_constraint(trailing, pltpu.HBM)
    own_strips, updated = pl.pallas_call(
        update_kernel,
        grid=(tiles,),
        in_specs=[
            smem,
            vmem,
            vmem,
            vmem,
            pl.BlockSpec((cols_count, 1, strip, NB), lambda t: (0, t, 0, 0)),
            pl.BlockSpec((1, NB, NB), lambda t: (t, 0, 0)),
        ],
        out_specs=[
            pl.BlockSpec((1, strip, NB), lambda t: (t, 0, 0)),
            pl.BlockSpec((1, NB, NB), lambda t: (t, 0, 0)),
        ],
        out_shape=[
            jax.ShapeDtypeStruct((tiles, strip, NB), BF16),
            jax.ShapeDtypeStruct((tiles, NB, NB), BF16),
        ],
        scratch_shapes=[pltpu.VMEM((NB, NB), BF16)] * 2,
        compiler_params=params,
        cost_estimate=pl.CostEstimate(flops=30 * NB**3, bytes_accessed=8 << 20, transcendentals=0),
    )(at, high, low, tile, gathered, trailing)

    return (
        own_factor.reshape(NB // rows_count, 1, NB // cols_count, 1),
        own_strips.reshape(tiles, 1, strip, NB),
        updated.reshape(tiles, 1, NB, 1, NB),
    )


def solution(mesh):
    in_specs = (P(None, "row", "col", None), P("row", "col"), P(None, "row", None, "col", None))
    out_specs = (
        P(None, "row", None, "col"),
        P(None, "row", "col", None),
        P(None, "row", None, "col", None),
    )
    return jax.shard_map(
        on_device, mesh=mesh, in_specs=in_specs, out_specs=out_specs, check_vma=False
    )
```

time: 111 us -> 107 us (0.964)
  blocking collectives: 27 us -> 0 us
  starting transfers between devices: 24.7 us -> 36.9 us
  waiting for transfers between devices: 11 us -> 21.5 us
  Pallas kernels: 26.9 us -> 29.2 us
  local copies, waits for them, and re-layouts: 6.1 us -> 4.11 us
    all_to_all x1 -> x0, blocking collectives: 27 us -> none  [to_all(): lax.all_to_all(jnp.broadcast_to(x[None], (count,) + x.shape), axis, 0, 0)]
    all_to_all x2 -> x3, starting transfers between devices: 18.8 us -> 34.5 us  [the longest x1 15.7 us: on_device(): lax.all_to_all(jnp.broadcast_to(own[None], (cols_count,) + own.shape), 'c...]
    all_to_all x2 -> x3, waiting for transfers between devices: 9.44 us -> 17.2 us  [the longest x1 11 us: on_device(): lax.all_to_all(jnp.broadcast_to(own[None], (cols_count,) + own.shape), 'c...]
    ppermute x2 -> x1, starting transfers between devices: 5.87 us -> 2.38 us  [on_device(): piece = lax.ppermute(panel[0], ('row', 'col'), pairs)]
    ppermute x2 -> x1, waiting for transfers between devices: 0.84 us -> 3.56 us  [on_device(): piece = lax.ppermute(panel[0], ('row', 'col'), pairs)]
    pallas_call x2 -> x3, Pallas kernels: 26.9 us -> 29.2 us  [the longest x1 19.9 us: on_device(): pl.pallas_call(factor_kernel, grid=(1,), in_specs=[smem, pl.BlockSpec(spr...]
    unnamed x4 -> x2, local copies, waits for them, and re-layouts: 1.79 us -> 0.01 us
    broadcast_in_dim x4 -> x3, local copies, waits for them, and re-layouts: 3.01 us -> 2.49 us  [the longest x2 1.4 us: on_device(): jnp.broadcast_to(own[None], (cols_count,) + own.shape)]
  transfers between devices with their start and end apart: 5 -> 5, of which waited for: 2 -> 3; matrix products, arithmetic and copies ran while one was open for 5% -> 4% of each run, Pallas kernels for 18% -> 20%
where the time goes in v2:
time: 107 us; the launch traced here: 106 us
  starting transfers between devices  36.9 us (34%)
  Pallas kernels  29.2 us (27%)
  waiting for transfers between devices  21.5 us (20%)
  between operations  14.1 us (13%)
  local copies, waits for them, and re-layouts  4.11 us (4%)
    pallas_call x1, Pallas kernels, on_device(): pl.pallas_call(factor_kernel, grid=(1,), in_specs=[smem, pl.BlockSpec(spr...  19.9 us
    all_to_all x1, starting transfers between devices, on_device(): lax.all_to_all(jnp.broadcast_to(own[None], (cols_count,) + own.shape), 'c...  15.7 us
    all_to_all x1, waiting for transfers between devices, on_device(): lax.all_to_all(jnp.broadcast_to(own[None], (cols_count,) + own.shape), 'c...  11 us
    all_to_all x1, starting transfers between devices, on_device(): lax.all_to_all(jnp.broadcast_to(piece[None], (rows_count,) + piece.shape)...  9.44 us
    all_to_all x1, starting transfers between devices, on_device(): spread = lax.all_to_all(folded, 'row', 0, 0)  9.34 us
    pallas_call x1, Pallas kernels, on_device(): pl.pallas_call(update_kernel, grid=(tiles,), in_specs=[smem, vmem, vmem,...  7.53 us
    all_to_all x1, waiting for transfers between devices, on_device(): spread = lax.all_to_all(folded, 'row', 0, 0)  6.23 us
    ppermute x1, waiting for transfers between devices, on_device(): piece = lax.ppermute(panel[0], ('row', 'col'), pairs)  3.56 us
  transfers between devices with their start and end apart: 5, of which 3 were waited for; matrix products, arithmetic and copies ran while one was open for 4% of the time, Pallas kernels for 20%

profile of v2, /device:TPU:1, one launch (start us, length us, event | category | flops | bytes accessed | tf_op | source)
XLA Modules:
  0.0 106.4 jit_solution(13258310972830681221)
XLA Ops:
  7.2 0.0 all-gather.3.cloned.1.call-start
  7.2 0.7 all-gather.3.cloned.1.call-update
  7.9 0.8 broadcast_in_dim.6
  8.7 0.6 broadcast_in_dim.14
  9.3 15.7 %all-to-all-start = ((f32[16,4,128]{2,1,0:T(4,128)}), f32[16,4,128]{2,1,0:T(4,128)S(1)}, u32[]{:S(2)}, u32[]{:S(2)}) async-start(f32[16,4,128]{2,1,0:T(4,128)} %broadcast_in_dim.14), calls=%async_computation | async-start | bytes 65536 | tf_op jit(solution)/shard_map/all_to_all | solution.py:220
  25.1 0.6 pad_add_fusion.at_ref
  25.6 11.0 %all-to-all-done = f32[16,4,128]{2,1,0:T(4,128)S(1)} async-done(((f32[16,4,128]{2,1,0:T(4,128)}), f32[16,4,128]{2,1,0:T(4,128)S(1)}, u32[]{:S(2)}, u32[]{:S(2)}) %all-to-all-start) | async-done | bytes 32800 | tf_op jit(solution)/shard_map/all_to_all | solution.py:220
  36.6 0.1 reshape.29
  36.8 0.7 reshape.30.band_ref
  37.5 1.8 %shard_map.58 = bf16[32,16,640]{2,1,0:T(8,128)(2,1)} custom-call(s32[2]{0:T(128)} %pad_add_fusion.at_ref, f32[16,512]{1,0:T(8,128)} %reshape.30.band_ref), custom_call_target="tpu_custom_call" | custom-call | tf_op jit(solution)/shard_map/pallas_call | solution.py:224
  39.3 0.0 copy-start
  39.3 9.3 %all-to-all-start.1 = ((bf16[32,16,640]{2,1,0:T(8,128)(2,1)}), bf16[32,16,640]{2,1,0:T(8,128)(2,1)S(1)}, u32[]{:S(2)}, u32[]{:S(2)}) async-start(bf16[32,16,640]{2,1,0:T(8,128)(2,1)} %shard_map.58), calls=%async_computation.1 | async-start | bytes 1310720 | tf_op jit(solution)/shard_map/all_to_all | solution.py:230
  48.6 0.8 slice_bitcast_fusion
  49.4 2.4 %collective-permute-start = (bf16[32,512]{1,0:T(8,128)(2,1)S(1)}, bf16[32,512]{1,0:T(8,128)(2,1)S(1)}, u32[]{:S(2)}, u32[]{:S(2)}) collective-permute-start(bf16[32,512]{1,0:T(8,128)(2,1)S(1)} %slice_bitcast_fusion), channel_id=1, source_target_pairs={{0,0},{1,16},{2,32},{3,48},{4,64},{5,80},{6,96},{7,112},{8,128},{9... | collective-permute-start | bytes 98312 | tf_op jit(solution)/shard_map/ppermute | solution.py:216
  51.8 3.6 %collective-permute-done = bf16[32,512]{1,0:T(8,128)(2,1)S(1)} collective-permute-done((bf16[32,512]{1,0:T(8,128)(2,1)S(1)}, bf16[32,512]{1,0:T(8,128)(2,1)S(1)}, u32[]{:S(2)}, u32[]{:S(2)}) %collective-permute-start) | collective-permute-done | bytes 32800 | tf_op jit(solution)/shard_map/ppermute | solution.py:216
  55.3 6.2 %all-to-all-done.1.spread_ref = bf16[32,16,640]{2,1,0:T(8,128)(2,1)S(1)} async-done(((bf16[32,16,640]{2,1,0:T(8,128)(2,1)}), bf16[32,16,640]{2,1,0:T(8,128)(2,1)S(1)}, u32[]{:S(2)}, u32[]{:S(2)}) %all-to-all-start.1) | async-done | bytes 655392 | tf_op jit(solution)/shard_map/all_to_all | solution.py:230
  61.6 1.1 %broadcast_in_dim.15 = bf16[32,32,512]{2,1,0:T(8,128)(2,1)} broadcast(bf16[32,512]{1,0:T(8,128)(2,1)S(1)} %collective-permute-done), dimensions={1,2} | broadcast | bytes 1081344 | tf_op jit(solution)/shard_map/broadcast_in_dim | solution.py:232
  62.7 9.4 %all-to-all-start.2 = ((bf16[32,32,512]{2,1,0:T(8,128)(2,1)}), bf16[32,32,512]{2,1,0:T(8,128)(2,1)S(1)}, u32[]{:S(2)}, u32[]{:S(2)}) async-start(bf16[32,32,512]{2,1,0:T(8,128)(2,1)} %broadcast_in_dim.15), calls=%async_computation.2 | async-start | bytes 2097152 | tf_op jit(solution)/shard_map/all_to_all | solution.py:232
  72.1 0.0 copy-done
  72.1 19.9 %shard_map.59 = (f32[16,32]{1,0:T(8,128)}, bf16[512,512]{1,0:T(8,128)(2,1)S(1)}, bf16[512,512]{1,0:T(8,128)(2,1)S(1)}) custom-call(s32[2]{0:T(128)S(1)} %copy-done, bf16[32,16,640]{2,1,0:T(8,128)(2,1)S(1)} %all-to-all-done.1.spread_ref), custom_call_target="tpu_custom_call" | custom-call | flops 1610612736 | bytes 3145728 | tf_op jit(solution)/shard_map/pallas_call | solution.py:235
  92.0 0.0 all-to-all-done.2.tile_ref
  92.0 0.0 all-gather.3.cloned.1.call-done
  92.0 7.5 %shard_map.60 = (bf16[4,32,512]{2,1,0:T(8,128)(2,1)}, bf16[4,512,512]{2,1,0:T(8,128)(2,1)}) custom-call(s32[2]{0:T(128)S(1)} %copy-done, bf16[512,512]{1,0:T(8,128)(2,1)S(1)} %get-tuple-element.10.high_ref, bf16[512,512]{1,0:T(8,128)(2,1)S(1)} %get-tuple-element.11.low_ref, bf16[32,32,512]{2,1,0:T(8,128)(2,1)S(1)} %all-to-all-done.2.tile_ref, ...), custom_call_target="tpu_custom_call" | custom-call | flops 4026531840 | bytes 8388608 | tf_op jit(solution)/shard_map/pallas_call | solution.py:252
  (1 shorter events, 0.0 us)
Async XLA Ops:
  7.2 84.8 %all-gather.3.cloned.1.call-start = ((), (), s32[]{:S(2)}) async-start(), calls=%async_computation.3 | async-start | bytes 2228224 | tf_op jit(solution)/shard_map/all_gather | solution.py:213
  9.3 27.3 %all-to-all-start = ((f32[16,4,128]{2,1,0:T(4,128)}), f32[16,4,128]{2,1,0:T(4,128)S(1)}, u32[]{:S(2)}, u32[]{:S(2)}) async-start(f32[16,4,128]{2,1,0:T(4,128)} %broadcast_in_dim.14), calls=%async_computation | async-start | bytes 65536 | tf_op jit(solution)/shard_map/all_to_all | solution.py:220
  39.3 32.8 %copy-start = (s32[2]{0:T(128)S(1)}, s32[2]{0:T(128)}, u32[]{:S(2)}) copy-start(s32[2]{0:T(128)} %pad_add_fusion.at_ref) | copy-start | bytes 28
  39.3 22.3 %all-to-all-start.1 = ((bf16[32,16,640]{2,1,0:T(8,128)(2,1)}), bf16[32,16,640]{2,1,0:T(8,128)(2,1)S(1)}, u32[]{:S(2)}, u32[]{:S(2)}) async-start(bf16[32,16,640]{2,1,0:T(8,128)(2,1)} %shard_map.58), calls=%async_computation.1 | async-start | bytes 1310720 | tf_op jit(solution)/shard_map/all_to_all | solution.py:230
  49.4 5.9 %collective-permute-start = (bf16[32,512]{1,0:T(8,128)(2,1)S(1)}, bf16[32,512]{1,0:T(8,128)(2,1)S(1)}, u32[]{:S(2)}, u32[]{:S(2)}) collective-permute-start(bf16[32,512]{1,0:T(8,128)(2,1)S(1)} %slice_bitcast_fusion), channel_id=1, source_target_pairs={{0,0},{1,16},{2,32},{3,48},{4,64},{5,80},{6,96},{7,112},{8,128},{9... | collective-permute-start | bytes 98312 | tf_op jit(solution)/shard_map/ppermute | solution.py:216
  62.7 29.3 %all-to-all-start.2 = ((bf16[32,32,512]{2,1,0:T(8,128)(2,1)}), bf16[32,32,512]{2,1,0:T(8,128)(2,1)S(1)}, u32[]{:S(2)}, u32[]{:S(2)}) async-start(bf16[32,32,512]{2,1,0:T(8,128)(2,1)} %broadcast_in_dim.15), calls=%async_computation.2 | async-start | bytes 2097152 | tf_op jit(solution)/shard_map/all_to_all | solution.py:232
Sparse Core Ops, SparseCore 0:
  10.1 71.2 all-gather.2

commit v3 on v2

--- a/solution.py
+++ b/solution.py
@@ -8,6 +8,7 @@
 NB = 512
 BLOCK = 128
 LANES = 128
+FIRST = 1
 F32, BF16 = jnp.float32, jnp.bfloat16
 NT = (((1,), (1,)), ((), ()))
 NN = (((1,), (0,)), ((), ()))
@@ -123,53 +124,82 @@
         out_ref[i] = block
 
 
-def unfold(spread_ref, work, folded):
+def unfold(spread_ref, folded):
     count, half, _ = spread_ref.shape
     window = NB // 2
     lane = lax.broadcasted_iota(jnp.int32, (half, LANES), 1)
     for r in range(count):
-        part = spread_ref[r].astype(F32)
+        part = spread_ref[r, :, : NB + LANES].astype(F32)
         end = part[:, NB:]
         end = jnp.where(lane < half, end + pltpu.roll(end, LANES - half, 1), 0.0)
         line = jnp.concatenate([part[:, :window] + part[:, window:NB], end, jnp.zeros_like(end)], 1)
         folded[half * r : half * (r + 1), :] = pltpu.roll(line, half * r, 1) if r else line
-    per_block = BLOCK // half
+
+
+def folded_block(folded, i, j, half):
+    count, per_block = NB // half, BLOCK // half
     row = lax.broadcasted_iota(jnp.int32, (BLOCK, BLOCK), 0) // half
     col = lax.broadcasted_iota(jnp.int32, (BLOCK, BLOCK), 1) // half
-    for i in range(NB // BLOCK):
-        for j in range(i + 1):
-            here, there = pl.ds(BLOCK * i, BLOCK), pl.ds(BLOCK * j, BLOCK)
-            gap = (i - j) * per_block
-            if gap - per_block + 1 >= count // 2:
-                work[here, there] = folded[here, there]
-                continue
-            block = folded[there, here].T
-            if i == j:
-                block = jnp.where(col >= row, folded[here, there], block)
-            elif gap + per_block - 1 >= count // 2:
-                block = jnp.where(row - col + gap >= count // 2, folded[here, there], block)
-            work[here, there] = block
-
-
-def factor_kernel(at_ref, spread_ref, own_ref, high_ref, low_ref, work, factor, inverse):
-    unfold(spread_ref, work, factor)
+    here, there = pl.ds(BLOCK * i, BLOCK), pl.ds(BLOCK * j, BLOCK)
+    gap = (i - j) * per_block
+    if gap - per_block + 1 >= count // 2:
+        return folded[here, there]
+    block = folded[there, here].T
+    if i == j:
+        return jnp.where(col >= row, folded[here, there], block)
+    if gap + per_block - 1 >= count // 2:
+        return jnp.where(row - col + gap >= count // 2, folded[here, there], block)
+    return block
+
+
+def factor_steps(steps, work, pending, factor, inverse):
+    blocks = NB // BLOCK
+    for p in steps:
+        here = pl.ds(BLOCK * p, BLOCK)
+        upper, block_inverse = factor_block(work[p, p])
+        below = {}
+        for q in range(p + 1, blocks):
+            below[q] = dot_split(work[q, p], block_inverse, NT)
+            for r in range(p + 1, q + 1):
+                work[q, r] = work[q, r] - dot_split(below[q], below[r], NT)
+        factor[here, here] = upper.T
+        rows = {r: dot_split(block_inverse, pending[p, r], NN) for r in range(p)}
+        rows[p] = block_inverse
+        for r in range(p + 1):
+            inverse[here, pl.ds(BLOCK * r, BLOCK)] = rows[r]
+        for q in range(p + 1, blocks):
+            factor[pl.ds(BLOCK * q, BLOCK), here] = below[q]
+            for r in range(p + 1):
+                change = dot_split(below[q], rows[r], NN)
+                pending[q, r] = pending[q, r] - change if r < p else -change
+
+
+def block_at(i, j):
+    return pl.ds(BLOCK * i, BLOCK), pl.ds(BLOCK * j, BLOCK)
+
+
+def first_kernel(spread_ref, factor, state, folded):
+    unfold(spread_ref, folded)
     factor[...] = jnp.zeros_like(factor)
-    inverse[...] = jnp.zeros_like(inverse)
-    for start in range(0, NB, BLOCK):
-        here = pl.ds(start, BLOCK)
-        before = pl.ds(0, start)
-        upto = pl.ds(0, start + BLOCK)
-        after = pl.ds(start + BLOCK, NB - start - BLOCK)
-        upper, block_inverse = factor_block(work[here, here])
-        factor[here, here] = upper.T
-        inverse[here, here] = block_inverse
-        if start:
-            inverse[here, before] = dot_split(block_inverse, inverse[here, before], NN)
-        if start + BLOCK < NB:
-            below = dot_split(work[after, here], block_inverse, NT)
-            factor[after, here] = below
-            work[after, after] = work[after, after] - dot_split(below, below, NT)
-            inverse[after, upto] = inverse[after, upto] - dot_split(below, inverse[here, upto], NN)
+    state[...] = jnp.zeros_like(state)
+    blocks = NB // BLOCK
+    half = spread_ref.shape[1]
+    work = {(i, j): folded_block(folded, i, j, half) for j in range(blocks) for i in range(j, blocks)}
+    pending = {}
+    factor_steps(range(FIRST), work, pending, factor, state)
+    for q in range(FIRST, blocks):
+        for r in range(q + 1):
+            state[block_at(q, r)] = pending[q, r] if r < FIRST else work[q, r]
+
+
+def second_kernel(at_ref, factor_ref, state_ref, own_ref, high_ref, low_ref, factor, inverse):
+    factor[...] = factor_ref[...]
+    inverse[...] = state_ref[...]
+    blocks = NB // BLOCK
+    todo = range(FIRST, blocks)
+    pending = {(q, r): state_ref[block_at(q, r)] for q in todo for r in range(FIRST)}
+    work = {(q, r): state_ref[block_at(q, r)] for r in todo for q in range(r, blocks)}
+    factor_steps(todo, work, pending, factor, inverse)
     high, low = split(inverse[...])
     high_ref[...] = high
     low_ref[...] = low
@@ -185,19 +215,22 @@
     own_ref[...] = picked[:, :count_b]
 
 
-def update_kernel(at_ref, high_ref, low_ref, tile_ref, panel_ref, trailing_ref, own_ref, out_ref, column, solved):
+def prepare_kernel(high_ref, low_ref, tile_ref, panel_ref, own_ref, out_high_ref, out_low_ref):
     high, low = high_ref[...], low_ref[...]
-
-    strip = own_ref.shape[1]
-
-    @pl.when(pl.program_id(0) == 0)
-    def _():
-        column[...] = solve(tile_ref[: NB // strip].reshape(NB, NB), high, low)
-
-    rows = solve(panel_ref[...].reshape(NB, NB), high, low)
-    solved[...] = rows
-    own_ref[0] = solved[pl.ds(pl.multiple_of(at_ref[1] * strip, strip), strip), :]
-    out_ref[0] = (trailing_ref[0].astype(F32) - dot(rows, column[...], NT)).astype(BF16)
+    tiles, strip, _ = panel_ref.shape
+    column = solve(tile_ref[: NB // strip].reshape(NB, NB), high, low)
+    own_ref[...] = solve(panel_ref[...].reshape(tiles * strip, NB), high, low).reshape(tiles, strip, NB)
+    out_high_ref[...], out_low_ref[...] = split(dot(column, high, NN) + dot(column, low, NN))
+
+
+def update_kernel(high_ref, low_ref, panel_ref, trailing_ref, out_ref):
+    rows = panel_ref[...].reshape(NB, NB)
+    product = dot(rows, high_ref[...], NT) + dot(rows, low_ref[...], NT)
+    out_ref[0] = (trailing_ref[0].astype(F32) - product).astype(BF16)
+
+
+def whole(x):
+    return pl.BlockSpec(x.shape, lambda i: (0,) * x.ndim)
 
 
 def on_device(panel, diagonal_tile, trailing):
@@ -228,50 +261,62 @@
         out_shape=jax.ShapeDtypeStruct((rows_count, half, NB + LANES), BF16),
     )(at, band)
     spread = lax.all_to_all(folded, "row", 0, 0)
-    piece = lax.optimization_barrier((piece, spread))[0]
+    params = pltpu.CompilerParams(vmem_limit_bytes=16 << 20)
+    full = jax.ShapeDtypeStruct((NB, NB), F32)
+    half_tile = jax.ShapeDtypeStruct((NB, NB), BF16)
+    cost = pl.CostEstimate(flops=6 * NB**3, bytes_accessed=3 << 20, transcendentals=0)
+    factor, state = pl.pallas_call(
+        first_kernel,
+        in_specs=[vmem],
+        out_specs=[vmem] * 2,
+        out_shape=[full] * 2,
+        scratch_shapes=[pltpu.VMEM((NB, NB), F32)],
+        compiler_params=params,
+        cost_estimate=cost,
+    )(spread)
+    piece, factor, state = lax.optimization_barrier((piece, factor, state))
     tile = lax.all_to_all(jnp.broadcast_to(piece[None], (rows_count,) + piece.shape), "row", 0, 0)
-
-    params = pltpu.CompilerParams(vmem_limit_bytes=32 << 20)
     own_factor, high, low = pl.pallas_call(
-        factor_kernel,
+        second_kernel,
         grid=(1,),
-        in_specs=[smem, pl.BlockSpec(spread.shape, lambda i: (0, 0, 0))],
+        in_specs=[smem, vmem, vmem],
         out_specs=[pl.BlockSpec((NB // rows_count, NB // cols_count), lambda i: (0, 0))]
         + [pl.BlockSpec((NB, NB), lambda i: (0, 0))] * 2,
         out_shape=[
             jax.ShapeDtypeStruct((NB // rows_count, NB // cols_count), F32),
-        ]
-        + [jax.ShapeDtypeStruct((NB, NB), BF16)] * 2,
-        scratch_shapes=[pltpu.VMEM((NB, NB), F32)] * 3,
+            half_tile,
+            half_tile,
+        ],
+        scratch_shapes=[pltpu.VMEM((NB, NB), F32)] * 2,
         compiler_params=params,
-        cost_estimate=pl.CostEstimate(flops=12 * NB**3, bytes_accessed=3 << 20, transcendentals=0),
-    )(at, spread)
-
+        cost_estimate=cost,
+    )(at, factor, state)
+
+    own_strips, high, low = pl.pallas_call(
+        prepare_kernel,
+        grid=(1,),
+        in_specs=[whole(high), whole(low), whole(tile), whole(panel)],
+        out_specs=[whole(panel), whole(high), whole(low)],
+        out_shape=[jax.ShapeDtypeStruct((tiles, strip, NB), BF16), half_tile, half_tile],
+        compiler_params=params,
+        cost_estimate=pl.CostEstimate(flops=10 * NB**3, bytes_accessed=3 << 20, transcendentals=0),
+    )(high, low, tile, panel)
     gathered = pltpu.with_memory_space_constraint(gathered, pltpu.HBM)
     trailing = pltpu.with_memory_space_constraint(trailing, pltpu.HBM)
-    own_strips, updated = pl.pallas_call(
+    updated = pl.pallas_call(
         update_kernel,
         grid=(tiles,),
         in_specs=[
-            smem,
-            vmem,
-            vmem,
-            vmem,
+            whole(high),
+            whole(low),
             pl.BlockSpec((cols_count, 1, strip, NB), lambda t: (0, t, 0, 0)),
             pl.BlockSpec((1, NB, NB), lambda t: (t, 0, 0)),
         ],
-        out_specs=[
-            pl.BlockSpec((1, strip, NB), lambda t: (t, 0, 0)),
-            pl.BlockSpec((1, NB, NB), lambda t: (t, 0, 0)),
-        ],
-        out_shape=[
-            jax.ShapeDtypeStruct((tiles, strip, NB), BF16),
-            jax.ShapeDtypeStruct((tiles, NB, NB), BF16),
-        ],
-        scratch_shapes=[pltpu.VMEM((NB, NB), BF16)] * 2,
+        out_specs=pl.BlockSpec((1, NB, NB), lambda t: (t, 0, 0)),
+        out_shape=jax.ShapeDtypeStruct((tiles, NB, NB), BF16),
         compiler_params=params,
-        cost_estimate=pl.CostEstimate(flops=30 * NB**3, bytes_accessed=8 << 20, transcendentals=0),
-    )(at, high, low, tile, gathered, trailing)
+        cost_estimate=pl.CostEstimate(flops=16 * NB**3, bytes_accessed=6 << 20, transcendentals=0),
+    )(high, low, gathered, trailing)
 
     return (
         own_factor.reshape(NB // rows_count, 1, NB // cols_count, 1),

time: 107 us -> 106 us (level)
  starting transfers between devices: 36.9 us -> 31.3 us
  local copies, waits for them, and re-layouts: 4.11 us -> 7.04 us
  waiting for transfers between devices: 21.5 us -> 23.3 us
    all_to_all x1, starting transfers between devices: 9.44 us -> 3.9 us  [on_device(): lax.all_to_all(jnp.broadcast_to(piece[None], (rows_count,) + piece.shape)...]
    all_to_all x1, waiting for transfers between devices: 6.23 us -> 10.5 us  [on_device(): spread = lax.all_to_all(folded, 'row', 0, 0)]
    unnamed x2 -> x12, local copies, waits for them, and re-layouts: 0.01 us -> 3.69 us
    ppermute x1, waiting for transfers between devices: 3.56 us -> 0.01 us  [on_device(): piece = lax.ppermute(panel[0], ('row', 'col'), pairs)]
    all_to_all x1, waiting for transfers between devices: 0.01 us -> 1.12 us  [on_device(): lax.all_to_all(jnp.broadcast_to(piece[None], (rows_count,) + piece.shape)...]
    pallas_call x2 -> x4, Pallas kernels: 27.4 us -> 27.5 us  [the longest x1 14 us: on_device(): pl.pallas_call(second_kernel, grid=(1,), in_specs=[smem, vmem, vmem], out...]
  transfers between devices with their start and end apart: 5 -> 5, of which waited for: 3 -> 3; matrix products, arithmetic and copies ran while one was open for 4% -> 4% of each run, Pallas kernels for 20% -> 22%
where the time goes in v3:
time: 106 us
  starting transfers between devices  31.3 us (30%)
  Pallas kernels  29.3 us (28%)
  waiting for transfers between devices  23.3 us (22%)
  between operations  14.1 us (13%)
  local copies, waits for them, and re-layouts  7.04 us (7%)
    all_to_all x1, starting transfers between devices, on_device(): lax.all_to_all(jnp.broadcast_to(own[None], (cols_count,) + own.shape), 'c...  15.7 us
    pallas_call x1, Pallas kernels, on_device(): pl.pallas_call(second_kernel, grid=(1,), in_specs=[smem, vmem, vmem], out...  14 us
    all_to_all x1, waiting for transfers between devices, on_device(): lax.all_to_all(jnp.broadcast_to(own[None], (cols_count,) + own.shape), 'c...  11 us
    all_to_all x1, waiting for transfers between devices, on_device(): spread = lax.all_to_all(folded, 'row', 0, 0)  10.5 us
    all_to_all x1, starting transfers between devices, on_device(): spread = lax.all_to_all(folded, 'row', 0, 0)  9.2 us
    pallas_call x1, Pallas kernels, on_device(): pl.pallas_call(first_kernel, in_specs=[vmem], out_specs=[vmem] * 2, out_s...  6.08 us
    pallas_call x1, Pallas kernels, on_device(): pl.pallas_call(update_kernel, grid=(tiles,), in_specs=[whole(high), whole...  5.73 us
    all_to_all x1, starting transfers between devices, on_device(): lax.all_to_all(jnp.broadcast_to(piece[None], (rows_count,) + piece.shape)...  3.9 us
  transfers between devices with their start and end apart: 5, of which 3 were waited for; matrix products, arithmetic and copies ran while one was open for 4% of the time, Pallas kernels for 22%

profile of v3, /device:TPU:1, one launch (start us, length us, event | category | flops | bytes accessed | tf_op | source)
XLA Modules:
  0.0 105.6 jit_solution(1115475518634196114)
XLA Ops:
  7.2 0.0 copy-start
  7.2 0.0 all-gather.3.cloned.1.call-start
  7.2 0.7 all-gather.3.cloned.1.call-update
  7.9 0.8 broadcast_in_dim.6
  8.7 0.6 broadcast_in_dim.14
  9.3 15.7 %all-to-all-start = ((f32[16,4,128]{2,1,0:T(4,128)}), f32[16,4,128]{2,1,0:T(4,128)S(1)}, u32[]{:S(2)}, u32[]{:S(2)}) async-start(f32[16,4,128]{2,1,0:T(4,128)} %broadcast_in_dim.14), calls=%async_computation | async-start | bytes 65536 | tf_op jit(solution)/shard_map/all_to_all | solution.py:253
  25.1 0.6 pad_add_fusion.at_ref
  25.6 11.0 %all-to-all-done = f32[16,4,128]{2,1,0:T(4,128)S(1)} async-done(((f32[16,4,128]{2,1,0:T(4,128)}), f32[16,4,128]{2,1,0:T(4,128)S(1)}, u32[]{:S(2)}, u32[]{:S(2)}) %all-to-all-start) | async-done | bytes 32800 | tf_op jit(solution)/shard_map/all_to_all | solution.py:253
  36.6 0.1 reshape.31
  36.8 0.7 reshape.32.band_ref
  37.5 1.8 %shard_map.58 = bf16[32,16,640]{2,1,0:T(8,128)(2,1)} custom-call(s32[2]{0:T(128)} %pad_add_fusion.at_ref, f32[16,512]{1,0:T(8,128)} %reshape.32.band_ref), custom_call_target="tpu_custom_call" | custom-call | tf_op jit(solution)/shard_map/pallas_call | solution.py:257
  39.3 9.2 %all-to-all-start.1 = ((bf16[32,16,640]{2,1,0:T(8,128)(2,1)}), bf16[32,16,640]{2,1,0:T(8,128)(2,1)S(1)}, u32[]{:S(2)}, u32[]{:S(2)}) async-start(bf16[32,16,640]{2,1,0:T(8,128)(2,1)} %shard_map.58), calls=%async_computation.1 | async-start | bytes 1310720 | tf_op jit(solution)/shard_map/all_to_all | solution.py:263
  48.5 0.0 copy-done
  48.5 2.4 %collective-permute-start = (bf16[32,512]{1,0:T(8,128)(2,1)S(1)}, bf16[32,512]{1,0:T(8,128)(2,1)S(1)}, u32[]{:S(2)}, u32[]{:S(2)}) collective-permute-start(bf16[32,512]{1,0:T(8,128)(2,1)S(1)} %slice_bitcast_fusion), channel_id=1, source_target_pairs={{0,0},{1,16},{2,32},{3,48},{4,64},{5,80},{6,96},{7,112},{8,128},{9... | collective-permute-start | bytes 98312 | tf_op jit(solution)/shard_map/ppermute | solution.py:249
  50.9 10.5 %all-to-all-done.1.spread_ref = bf16[32,16,640]{2,1,0:T(8,128)(2,1)S(1)} async-done(((bf16[32,16,640]{2,1,0:T(8,128)(2,1)}), bf16[32,16,640]{2,1,0:T(8,128)(2,1)S(1)}, u32[]{:S(2)}, u32[]{:S(2)}) %all-to-all-start.1) | async-done | bytes 655392 | tf_op jit(solution)/shard_map/all_to_all | solution.py:263
  61.4 6.1 %shard_map.59 = (f32[512,512]{1,0:T(8,128)S(1)}, f32[512,512]{1,0:T(8,128)S(1)}) custom-call(bf16[32,16,640]{2,1,0:T(8,128)(2,1)S(1)} %all-to-all-done.1.spread_ref), custom_call_target="tpu_custom_call" | custom-call | flops 805306368 | bytes 3145728 | tf_op jit(solution)/shard_map/pallas_call | solution.py:268
  67.5 0.0 copy-start.1
  67.5 0.0 collective-permute-done
  67.5 1.1 %broadcast_in_dim.15 = bf16[32,32,512]{2,1,0:T(8,128)(2,1)} broadcast(bf16[32,512]{1,0:T(8,128)(2,1)S(1)} %collective-permute-done), dimensions={1,2} | broadcast | bytes 1081344 | tf_op jit(solution)/shard_map/broadcast_in_dim | solution.py:278
  68.6 3.9 %all-to-all-start.2 = ((bf16[32,32,512]{2,1,0:T(8,128)(2,1)}), bf16[32,32,512]{2,1,0:T(8,128)(2,1)S(1)}, u32[]{:S(2)}, u32[]{:S(2)}) async-start(bf16[32,32,512]{2,1,0:T(8,128)(2,1)} %broadcast_in_dim.15), calls=%async_computation.2 | async-start | bytes 2097152 | tf_op jit(solution)/shard_map/all_to_all | solution.py:278
  72.5 0.0 copy-done.1
  72.5 14.0 %shard_map.60 = (f32[16,32]{1,0:T(8,128)}, bf16[512,512]{1,0:T(8,128)(2,1)S(1)}, bf16[512,512]{1,0:T(8,128)(2,1)S(1)}) custom-call(s32[2]{0:T(128)S(1)} %copy-done.1, f32[512,512]{1,0:T(8,128)S(1)} %get-tuple-element.16.factor_ref, f32[512,512]{1,0:T(8,128)S(1)} %get-tuple-element.17.state_ref), custom_call_target="tpu_custom_call" | custom-call | flops 805306368 | bytes 3145728 | tf_op jit(solution)/shard_map/pallas_call | solution.py:279
  86.5 0.0 copy-start.2
  86.5 0.8 copy-done.2
  87.3 0.0 copy-start.4
  87.3 0.8 copy-done.4
  88.1 1.1 %all-to-all-done.2.tile_ref = bf16[32,32,512]{2,1,0:T(8,128)(2,1)S(1)} async-done(((bf16[32,32,512]{2,1,0:T(8,128)(2,1)}), bf16[32,32,512]{2,1,0:T(8,128)(2,1)S(1)}, u32[]{:S(2)}, u32[]{:S(2)}) %all-to-all-start.2) | async-done | bytes 1048608 | tf_op jit(solution)/shard_map/all_to_all | solution.py:278
  89.3 0.0 copy-start.3
  89.3 1.0 copy-done.3
  90.3 0.0 copy-start.5
  90.3 1.0 copy-done.5
  91.3 1.7 %shard_map.61 = (bf16[4,32,512]{2,1,0:T(8,128)(2,1)}, bf16[512,512]{1,0:T(8,128)(2,1)S(1)}, bf16[512,512]{1,0:T(8,128)(2,1)S(1)}) custom-call(bf16[512,512]{1,0:T(8,128)(2,1)S(1)} %copy-done.3, bf16[512,512]{1,0:T(8,128)(2,1)S(1)} %copy-done.5, bf16[32,32,512]{2,1,0:T(8,128)(2,1)S(1)} %all-to-all-done.2.tile_ref, bf16[4,32,512]{2,1,0:T(8,128)(2,1)S(1)} %bitcast.17), custom_call_target="tpu_custom_call" | custom-call | flops 1342177280 | bytes 3145728 | tf_op jit(solution)/shard_map/pallas_call | solution.py:295
  93.0 0.0 all-gather.3.cloned.1.call-done
  93.1 5.7 %shard_map.62 = bf16[4,512,512]{2,1,0:T(8,128)(2,1)} custom-call(bf16[512,512]{1,0:T(8,128)(2,1)S(1)} %get-tuple-element.23.high_ref, bf16[512,512]{1,0:T(8,128)(2,1)S(1)} %get-tuple-element.24.low_ref, bf16[16,4,32,512]{3,2,1,0:T(8,128)(2,1)} %bitcast.20, bf16[4,512,512]{2,1,0:T(8,128)(2,1)} %bitcast.19), custom_call_target="tpu_custom_call" | custom-call | flops 2147483648 | bytes 6291456 | tf_op jit(solution)/shard_map/pallas_call | solution.py:306
  (2 shorter events, 0.0 us)
Async XLA Ops:
  7.2 41.3 %copy-start = (bf16[4,1,32,512]{3,2,1,0:T(8,128)(2,1)S(1)}, bf16[4,1,32,512]{3,2,1,0:T(8,128)(2,1)}, u32[]{:S(2)}) copy-start(bf16[4,1,32,512]{3,2,1,0:T(8,128)(2,1)} %param.3) | copy-start | bytes 393220
  7.2 85.9 %all-gather.3.cloned.1.call-start = ((), (), s32[]{:S(2)}) async-start(), calls=%async_computation.3 | async-start | bytes 2228224 | tf_op jit(solution)/shard_map/all_gather | solution.py:246
  9.3 27.3 %all-to-all-start = ((f32[16,4,128]{2,1,0:T(4,128)}), f32[16,4,128]{2,1,0:T(4,128)S(1)}, u32[]{:S(2)}, u32[]{:S(2)}) async-start(f32[16,4,128]{2,1,0:T(4,128)} %broadcast_in_dim.14), calls=%async_computation | async-start | bytes 65536 | tf_op jit(solution)/shard_map/all_to_all | solution.py:253
  39.3 22.1 %all-to-all-start.1 = ((bf16[32,16,640]{2,1,0:T(8,128)(2,1)}), bf16[32,16,640]{2,1,0:T(8,128)(2,1)S(1)}, u32[]{:S(2)}, u32[]{:S(2)}) async-start(bf16[32,16,640]{2,1,0:T(8,128)(2,1)} %shard_map.58), calls=%async_computation.1 | async-start | bytes 1310720 | tf_op jit(solution)/shard_map/all_to_all | solution.py:263
  48.5 19.0 %collective-permute-start = (bf16[32,512]{1,0:T(8,128)(2,1)S(1)}, bf16[32,512]{1,0:T(8,128)(2,1)S(1)}, u32[]{:S(2)}, u32[]{:S(2)}) collective-permute-start(bf16[32,512]{1,0:T(8,128)(2,1)S(1)} %slice_bitcast_fusion), channel_id=1, source_target_pairs={{0,0},{1,16},{2,32},{3,48},{4,64},{5,80},{6,96},{7,112},{8,128},{9... | collective-permute-start | bytes 98312 | tf_op jit(solution)/shard_map/ppermute | solution.py:249
  67.5 5.0 %copy-start.1 = (s32[2]{0:T(128)S(1)}, s32[2]{0:T(128)}, u32[]{:S(2)}) copy-start(s32[2]{0:T(128)} %pad_add_fusion.at_ref) | copy-start | bytes 28
  68.6 20.6 %all-to-all-start.2 = ((bf16[32,32,512]{2,1,0:T(8,128)(2,1)}), bf16[32,32,512]{2,1,0:T(8,128)(2,1)S(1)}, u32[]{:S(2)}, u32[]{:S(2)}) async-start(bf16[32,32,512]{2,1,0:T(8,128)(2,1)} %broadcast_in_dim.15), calls=%async_computation.2 | async-start | bytes 2097152 | tf_op jit(solution)/shard_map/all_to_all | solution.py:278
  86.5 0.8 copy-start.2
  87.3 0.8 copy-start.4
  89.3 1.0 copy-start.3
  90.3 1.0 copy-start.5
Sparse Core Ops, SparseCore 0:
  10.1 72.2 all-gather.2

commit v4 on v3

--- a/solution.py
+++ b/solution.py
@@ -291,6 +291,7 @@
         compiler_params=params,
         cost_estimate=cost,
     )(at, factor, state)
+    high, low = (pltpu.with_memory_space_constraint(x, pltpu.HBM) for x in (high, low))
 
     own_strips, high, low = pl.pallas_call(
         prepare_kernel,

time: 106 us -> 105 us (level)
  local copies, waits for them, and re-layouts: 7.04 us -> 4.98 us
  Pallas kernels: 29.3 us -> 30.5 us
    unnamed x12 -> x8, local copies, waits for them, and re-layouts: 3.69 us -> 1.63 us
    pallas_call x1, Pallas kernels: 1.7 us -> 2.89 us  [on_device(): pl.pallas_call(prepare_kernel, grid=(1,), in_specs=[whole(high), whole(lo...]
  transfers between devices with their start and end apart: 5 -> 5, of which waited for: 3 -> 3; matrix products, arithmetic and copies ran while one was open for 4% -> 4% of each run, Pallas kernels for 22% -> 24%
where the time goes in v4:
time: 105 us
  starting transfers between devices  31.3 us (30%)
  Pallas kernels  30.5 us (29%)
  waiting for transfers between devices  23.3 us (22%)
  between operations  14.1 us (13%)
  local copies, waits for them, and re-layouts  4.98 us (5%)
    all_to_all x1, starting transfers between devices, on_device(): lax.all_to_all(jnp.broadcast_to(own[None], (cols_count,) + own.shape), 'c...  15.7 us
    pallas_call x1, Pallas kernels, on_device(): pl.pallas_call(second_kernel, grid=(1,), in_specs=[smem, vmem, vmem], out...  14 us
    all_to_all x1, waiting for transfers between devices, on_device(): lax.all_to_all(jnp.broadcast_to(own[None], (cols_count,) + own.shape), 'c...  11 us
    all_to_all x1, waiting for transfers between devices, on_device(): spread = lax.all_to_all(folded, 'row', 0, 0)  10.5 us
    all_to_all x1, starting transfers between devices, on_device(): spread = lax.all_to_all(folded, 'row', 0, 0)  9.2 us
    pallas_call x1, Pallas kernels, on_device(): pl.pallas_call(first_kernel, in_specs=[vmem], out_specs=[vmem] * 2, out_s...  6.08 us
    pallas_call x1, Pallas kernels, on_device(): pl.pallas_call(update_kernel, grid=(tiles,), in_specs=[whole(high), whole...  5.72 us
    all_to_all x1, starting transfers between devices, on_device(): lax.all_to_all(jnp.broadcast_to(piece[None], (rows_count,) + piece.shape)...  3.9 us
  transfers between devices with their start and end apart: 5, of which 3 were waited for; matrix products, arithmetic and copies ran while one was open for 4% of the time, Pallas kernels for 24%

profile of v4, /device:TPU:1, one launch (start us, length us, event | category | flops | bytes accessed | tf_op | source)
XLA Modules:
  0.0 104.7 jit_solution(12254699290153439542)
XLA Ops:
  7.2 0.0 copy-start
  7.2 0.0 all-gather.3.cloned.1.call-start
  7.2 0.7 all-gather.3.cloned.1.call-update
  7.9 0.8 broadcast_in_dim.6
  8.7 0.6 broadcast_in_dim.14
  9.3 15.7 %all-to-all-start = ((f32[16,4,128]{2,1,0:T(4,128)}), f32[16,4,128]{2,1,0:T(4,128)S(1)}, u32[]{:S(2)}, u32[]{:S(2)}) async-start(f32[16,4,128]{2,1,0:T(4,128)} %broadcast_in_dim.14), calls=%async_computation | async-start | bytes 65536 | tf_op jit(solution)/shard_map/all_to_all | solution.py:253
  25.1 0.6 pad_add_fusion.at_ref
  25.7 11.0 %all-to-all-done = f32[16,4,128]{2,1,0:T(4,128)S(1)} async-done(((f32[16,4,128]{2,1,0:T(4,128)}), f32[16,4,128]{2,1,0:T(4,128)S(1)}, u32[]{:S(2)}, u32[]{:S(2)}) %all-to-all-start) | async-done | bytes 32800 | tf_op jit(solution)/shard_map/all_to_all | solution.py:253
  36.6 0.1 reshape.31
  36.8 0.7 reshape.32.band_ref
  37.5 1.8 %shard_map.58 = bf16[32,16,640]{2,1,0:T(8,128)(2,1)} custom-call(s32[2]{0:T(128)} %pad_add_fusion.at_ref, f32[16,512]{1,0:T(8,128)} %reshape.32.band_ref), custom_call_target="tpu_custom_call" | custom-call | tf_op jit(solution)/shard_map/pallas_call | solution.py:257
  39.3 9.2 %all-to-all-start.1 = ((bf16[32,16,640]{2,1,0:T(8,128)(2,1)}), bf16[32,16,640]{2,1,0:T(8,128)(2,1)S(1)}, u32[]{:S(2)}, u32[]{:S(2)}) async-start(bf16[32,16,640]{2,1,0:T(8,128)(2,1)} %shard_map.58), calls=%async_computation.1 | async-start | bytes 1310720 | tf_op jit(solution)/shard_map/all_to_all | solution.py:263
  48.5 0.0 copy-done
  48.5 2.4 %collective-permute-start = (bf16[32,512]{1,0:T(8,128)(2,1)S(1)}, bf16[32,512]{1,0:T(8,128)(2,1)S(1)}, u32[]{:S(2)}, u32[]{:S(2)}) collective-permute-start(bf16[32,512]{1,0:T(8,128)(2,1)S(1)} %slice_bitcast_fusion), channel_id=1, source_target_pairs={{0,0},{1,16},{2,32},{3,48},{4,64},{5,80},{6,96},{7,112},{8,128},{9... | collective-permute-start | bytes 98312 | tf_op jit(solution)/shard_map/ppermute | solution.py:249
  50.9 10.5 %all-to-all-done.1.spread_ref = bf16[32,16,640]{2,1,0:T(8,128)(2,1)S(1)} async-done(((bf16[32,16,640]{2,1,0:T(8,128)(2,1)}), bf16[32,16,640]{2,1,0:T(8,128)(2,1)S(1)}, u32[]{:S(2)}, u32[]{:S(2)}) %all-to-all-start.1) | async-done | bytes 655392 | tf_op jit(solution)/shard_map/all_to_all | solution.py:263
  61.4 6.1 %shard_map.59 = (f32[512,512]{1,0:T(8,128)S(1)}, f32[512,512]{1,0:T(8,128)S(1)}) custom-call(bf16[32,16,640]{2,1,0:T(8,128)(2,1)S(1)} %all-to-all-done.1.spread_ref), custom_call_target="tpu_custom_call" | custom-call | flops 805306368 | bytes 3145728 | tf_op jit(solution)/shard_map/pallas_call | solution.py:268
  67.5 0.0 copy-start.1
  67.5 0.0 collective-permute-done
  67.5 1.1 %broadcast_in_dim.15 = bf16[32,32,512]{2,1,0:T(8,128)(2,1)} broadcast(bf16[32,512]{1,0:T(8,128)(2,1)S(1)} %collective-permute-done), dimensions={1,2} | broadcast | bytes 1081344 | tf_op jit(solution)/shard_map/broadcast_in_dim | solution.py:278
  68.6 3.9 %all-to-all-start.2 = ((bf16[32,32,512]{2,1,0:T(8,128)(2,1)}), bf16[32,32,512]{2,1,0:T(8,128)(2,1)S(1)}, u32[]{:S(2)}, u32[]{:S(2)}) async-start(bf16[32,32,512]{2,1,0:T(8,128)(2,1)} %broadcast_in_dim.15), calls=%async_computation.2 | async-start | bytes 2097152 | tf_op jit(solution)/shard_map/all_to_all | solution.py:278
  72.5 0.0 copy-done.1
  72.5 14.0 %shard_map.60 = (f32[16,32]{1,0:T(8,128)}, bf16[512,512]{1,0:T(8,128)(2,1)S(1)}, bf16[512,512]{1,0:T(8,128)(2,1)S(1)}) custom-call(s32[2]{0:T(128)S(1)} %copy-done.1, f32[512,512]{1,0:T(8,128)S(1)} %get-tuple-element.16.factor_ref, f32[512,512]{1,0:T(8,128)S(1)} %get-tuple-element.17.state_ref), custom_call_target="tpu_custom_call" | custom-call | flops 805306368 | bytes 3145728 | tf_op jit(solution)/shard_map/pallas_call | solution.py:279
  86.5 0.0 copy-start.2
  86.5 0.8 copy-done.2
  87.4 0.0 copy-start.3
  87.4 0.8 copy-done.3
  88.2 1.1 %all-to-all-done.2.tile_ref = bf16[32,32,512]{2,1,0:T(8,128)(2,1)S(1)} async-done(((bf16[32,32,512]{2,1,0:T(8,128)(2,1)}), bf16[32,32,512]{2,1,0:T(8,128)(2,1)S(1)}, u32[]{:S(2)}, u32[]{:S(2)}) %all-to-all-start.2) | async-done | bytes 1048608 | tf_op jit(solution)/shard_map/all_to_all | solution.py:278
  89.3 2.9 %shard_map.61 = (bf16[4,32,512]{2,1,0:T(8,128)(2,1)}, bf16[512,512]{1,0:T(8,128)(2,1)S(1)}, bf16[512,512]{1,0:T(8,128)(2,1)S(1)}) custom-call(bf16[512,512]{1,0:T(8,128)(2,1)} %copy-done.2, bf16[512,512]{1,0:T(8,128)(2,1)} %copy-done.3, bf16[32,32,512]{2,1,0:T(8,128)(2,1)S(1)} %all-to-all-done.2.tile_ref, bf16[4,32,512]{2,1,0:T(8,128)(2,1)S(1)} %bitcast.17), custom_call_target="tpu_custom_call" | custom-call | flops 1342177280 | bytes 3145728 | tf_op jit(solution)/shard_map/pallas_call | solution.py:296
  92.2 0.0 all-gather.3.cloned.1.call-done
  92.2 5.7 %shard_map.62 = bf16[4,512,512]{2,1,0:T(8,128)(2,1)} custom-call(bf16[512,512]{1,0:T(8,128)(2,1)S(1)} %get-tuple-element.23.high_ref, bf16[512,512]{1,0:T(8,128)(2,1)S(1)} %get-tuple-element.24.low_ref, bf16[16,4,32,512]{3,2,1,0:T(8,128)(2,1)} %bitcast.20, bf16[4,512,512]{2,1,0:T(8,128)(2,1)} %bitcast.19), custom_call_target="tpu_custom_call" | custom-call | flops 2147483648 | bytes 6291456 | tf_op jit(solution)/shard_map/pallas_call | solution.py:307
  (2 shorter events, 0.0 us)
Async XLA Ops:
  7.2 41.3 %copy-start = (bf16[4,1,32,512]{3,2,1,0:T(8,128)(2,1)S(1)}, bf16[4,1,32,512]{3,2,1,0:T(8,128)(2,1)}, u32[]{:S(2)}) copy-start(bf16[4,1,32,512]{3,2,1,0:T(8,128)(2,1)} %param.3) | copy-start | bytes 393220
  7.2 85.0 %all-gather.3.cloned.1.call-start = ((), (), s32[]{:S(2)}) async-start(), calls=%async_computation.3 | async-start | bytes 2228224 | tf_op jit(solution)/shard_map/all_gather | solution.py:246
  9.3 27.3 %all-to-all-start = ((f32[16,4,128]{2,1,0:T(4,128)}), f32[16,4,128]{2,1,0:T(4,128)S(1)}, u32[]{:S(2)}, u32[]{:S(2)}) async-start(f32[16,4,128]{2,1,0:T(4,128)} %broadcast_in_dim.14), calls=%async_computation | async-start | bytes 65536 | tf_op jit(solution)/shard_map/all_to_all | solution.py:253
  39.3 22.1 %all-to-all-start.1 = ((bf16[32,16,640]{2,1,0:T(8,128)(2,1)}), bf16[32,16,640]{2,1,0:T(8,128)(2,1)S(1)}, u32[]{:S(2)}, u32[]{:S(2)}) async-start(bf16[32,16,640]{2,1,0:T(8,128)(2,1)} %shard_map.58), calls=%async_computation.1 | async-start | bytes 1310720 | tf_op jit(solution)/shard_map/all_to_all | solution.py:263
  48.5 19.0 %collective-permute-start = (bf16[32,512]{1,0:T(8,128)(2,1)S(1)}, bf16[32,512]{1,0:T(8,128)(2,1)S(1)}, u32[]{:S(2)}, u32[]{:S(2)}) collective-permute-start(bf16[32,512]{1,0:T(8,128)(2,1)S(1)} %slice_bitcast_fusion), channel_id=1, source_target_pairs={{0,0},{1,16},{2,32},{3,48},{4,64},{5,80},{6,96},{7,112},{8,128},{9... | collective-permute-start | bytes 98312 | tf_op jit(solution)/shard_map/ppermute | solution.py:249
  67.5 5.0 %copy-start.1 = (s32[2]{0:T(128)S(1)}, s32[2]{0:T(128)}, u32[]{:S(2)}) copy-start(s32[2]{0:T(128)} %pad_add_fusion.at_ref) | copy-start | bytes 28
  68.6 20.6 %all-to-all-start.2 = ((bf16[32,32,512]{2,1,0:T(8,128)(2,1)}), bf16[32,32,512]{2,1,0:T(8,128)(2,1)S(1)}, u32[]{:S(2)}, u32[]{:S(2)}) async-start(bf16[32,32,512]{2,1,0:T(8,128)(2,1)} %broadcast_in_dim.15), calls=%async_computation.2 | async-start | bytes 2097152 | tf_op jit(solution)/shard_map/all_to_all | solution.py:278
  86.5 0.8 copy-start.2
  87.4 0.8 copy-start.3
Sparse Core Ops, SparseCore 0:
  10.1 72.2 all-gather.2
